TPU v7x, 512 devices: a whole 4x8x8 slice. The times are simulated.
512 devices in a mesh: context: 32 (over y, z_lo, core), tensor: 16 (over x, z_hi).
Axes of the slice: x: 4, y: 8, z: 8 (z_hi: 4, z_lo: 2; z = z_hi * 2 + z_lo), core: 2. Of those that a mesh axis runs over, the one named last changes fastest.
Arguments:
- block_input: bfloat16 [4096, 8192], P(('context', 'tensor')), may hold values from -2 to 2
- norm_scale_weight: float32 [8192], replicated, may hold values from 0.1 to 1.9
- kv_weight: bfloat16 [8192, 2048], P('context', 'tensor'), may hold values from -0.0625 to 0.0625
- q_weight: bfloat16 [8192, 4096], P('context', 'tensor'), may hold values from -0.0625 to 0.0625
- kv_cotangent: bfloat16 [4096, 16, 256], P('context', 'tensor'), may hold values from -0.09375 to 0.09375
- q_cotangent: bfloat16 [4096, 4096], P('context', 'tensor'), may hold values from -0.09375 to 0.09375
Outputs:
- input_gradient: bfloat16 [4096, 8192], P(('context', 'tensor'))
- grad_weight: float32 [8192, 2048], P('context', 'tensor')
- grad_q_weight: float32 [8192, 4096], P('context', 'tensor')
All inputs are finite; a program needn't handle non-finite values.
Results may differ from a plain program's by a relative error of at most 0.019.
Values may be sent and summed in bfloat16 or wider, within the bound.
A program may use at most 64 MiB of HBM per device.

v0:
```python
import jax
import jax.numpy as jnp
from jax import lax
from jax.sharding import PartitionSpec as P


def partner_2(value, axis, bit):
    return lax.ppermute(value, axis, [(i, i ^ 1 << bit) for i in range(lax.axis_size(axis))])


def norm_moments(inputs):
    input_single32 = inputs.astype(jnp.float32)
    inverse_root_scale = lax.rsqrt(
        jnp.mean(input_single32 * input_single32, axis=-1, keepdims=True) + 1e-06
    )
    return (inverse_root_scale, input_single32 * inverse_root_scale)


def on_device(block_input, norm_scale_weight, kv_weight, q_weight, kv_cotangent, q_cotangent):
    local_inverse_scale, local_unit_rows = norm_moments(block_input)
    collected_rows = lax.all_gather(block_input, "tensor", axis=0, tiled=True)
    group_inverse_scale, group_unit_rows = norm_moments(collected_rows)
    normalized_rows = (group_unit_rows * norm_scale_weight).astype(jnp.bfloat16)
    width = kv_weight.shape[1]
    parity = lax.axis_index("tensor") % 2
    cotangent = kv_cotangent[:, 0, :]
    keys_part = cotangent[:, :width]
    values_part = cotangent[:, width:]
    own_half = jnp.where(parity == 0, keys_part, values_part)
    partner = partner_2(cotangent, "tensor", 0)
    other_half = jnp.where(parity == 0, partner[:, :width], partner[:, width:])
    head_grad = (own_half.astype(jnp.float32) + other_half.astype(jnp.float32)).astype(jnp.bfloat16)
    joint_grad = jnp.concatenate([head_grad, q_cotangent], axis=1)
    joint_weight = jnp.concatenate([kv_weight, q_weight], axis=1)
    partials = lax.dot_general(
        joint_grad,
        lax.all_gather(joint_weight, "context", axis=0, tiled=True),
        (((1,), (1,)), ((), ())),
        preferred_element_type=jnp.float32,
    )
    normed_grad = lax.psum_scatter(
        partials.astype(jnp.bfloat16), "tensor", scatter_dimension=0, tiled=True
    ).astype(jnp.float32)
    gain_scaled_rows = norm_scale_weight * normed_grad
    input_gradient = local_inverse_scale * (
        gain_scaled_rows
        - local_unit_rows * jnp.mean(gain_scaled_rows * local_unit_rows, axis=-1, keepdims=True)
    )
    regrouped = lax.all_to_all(normalized_rows, "context", split_axis=1, concat_axis=0, tiled=True)
    joint_result = lax.dot_general(
        regrouped,
        lax.all_gather(joint_grad, "context", axis=0, tiled=True),
        (((0,), (0,)), ((), ())),
        preferred_element_type=jnp.float32,
    )
    return (input_gradient.astype(jnp.bfloat16), joint_result[:, :width], joint_result[:, width:])


def solution(mesh):
    in_specs = (
        P(("context", "tensor"), None),
        P(),
        P("context", "tensor"),
        P("context", "tensor"),
        P("context", "tensor", None),
        P("context", "tensor"),
    )
    out_specs = (P(("context", "tensor"), None), P("context", "tensor"), P("context", "tensor"))
    return jax.shard_map(
        on_device, mesh=mesh, in_specs=in_specs, out_specs=out_specs, check_vma=False
    )
```

profile of v0, /device:TPU:1, one launch (start us, length us, event | category | flops | bytes accessed | tf_op | source)
XLA Modules:
  0.0 363.9 jit_solution(1859466576771635995)
XLA Ops:
  7.2 0.0 all-gather.6.cloned.1.call-start
  7.2 0.7 all-gather.6.cloned.1.call-update
  7.9 0.0 all-gather.4.cloned.1.call-start
  7.9 1.6 pad_maximum_fusion
  9.6 0.0 all-gather.4.cloned.1.call-update
  9.6 0.0 all-gather.8.cloned.1.call-start
  9.6 6.6 %collective-permute-start = (bf16[128,256]{1,0:T(8,128)(2,1)}, bf16[128,256]{1,0:T(8,128)(2,1)S(1)}, u32[]{:S(2)}, u32[]{:S(2)}) collective-permute-start(bf16[128,256]{1,0:T(8,128)(2,1)} %bitcast.10), channel_id=1, source_target_pairs={{0,1},{1,0},{2,3},{3,2},{4,5},{5,4},{6,7},{7,6},{8,9},{9,8},{10,11... | collective-permute-start | bytes 196616 | tf_op jit(solution)/shard_map/ppermute | solution.py:8
  16.3 1.8 collective-permute-done
  18.1 0.8 add_convert_fusion
  18.9 1.5 pad_maximum_fusion.1
  20.4 0.0 all-gather.8.cloned.1.call-update
  20.4 0.0 copy-start.1
  20.5 60.5 %all-gather.6.cloned.1.call-done = bf16[128,8192]{1,0:T(8,128)(2,1)} async-done(((bf16[8,8192]{1,0:T(8,128)(2,1)}), bf16[128,8192]{1,0:T(8,128)(2,1)}) %all-gather.6.cloned.1.call-update) | async-done | bytes 2097168 | tf_op jit(solution)/shard_map/all_gather | solution.py:21
  81.0 3.2 copy.11
  84.2 1.1 fusion
  85.3 4.4 %fusion.2 = bf16[128,8192]{0,1:T(8,128)(2,1)} fusion(bf16[128,8192]{0,1:T(8,128)(2,1)S(1)} %copy.11, f32[8192]{0:T(1024)S(1)} %copy-done.1, f32[128]{0:T(128)S(1)} %add_rsqrt_fusion), kind=kLoop, calls=%fused_computation.5 | loop fusion | flops 4194304 | bytes 4227584 | tf_op jit(solution)/shard_map/convert_element_type | solution.py:23
  89.7 8.7 %all-to-all-start = ((bf16[128,32,256]{0,2,1:T(8,128)(2,1)}), bf16[128,32,256]{0,2,1:T(8,128)(2,1)S(1)}, u32[]{:S(2)}, u32[]{:S(2)}) async-start(bf16[128,32,256]{0,2,1:T(8,128)(2,1)} %bitcast.8), calls=%async_computation.1 | async-start | bytes 4194304 | tf_op jit(solution)/shard_map/all_to_all | solution.py:49
  98.4 0.0 copy-start
  98.4 0.0 reduce-scatter.2.cloned.1.call-start
  98.5 88.1 %all-gather.4.cloned.1.call-done = bf16[8192,384]{1,0:T(8,128)(2,1)} async-done(((bf16[256,384]{1,0:T(8,128)(2,1)}), bf16[8192,384]{1,0:T(8,128)(2,1)}) %all-gather.4.cloned.1.call-update) | async-done | bytes 6291472 | tf_op jit(solution)/shard_map/all_gather | solution.py:37
  186.6 6.2 %convolution_convert_fusion = bf16[128,8192]{1,0:T(8,128)(2,1)} fusion(bf16[8192,384]{1,0:T(8,128)(2,1)} %all-gather.4.cloned.1.call-done, bf16[128,256]{1,0:T(8,128)(2,1)S(1)} %copy-done.2, bf16[128,128]{1,0:T(8,128)(2,1)S(1)} %add_convert_fusion), kind=kOutput, calls=%fused_computation | convolution fusion | flops 806551552 | bytes 8486912 | tf_op jit(solution)/shard_map/dot_general | solution.py:35
  192.7 0.0 reduce-scatter.2.cloned.1.call-update
  192.8 0.2 fusion.9
  193.0 0.0 all-to-all-done
  193.0 2.9 copy.12
  195.9 61.6 %all-gather.8.cloned.1.call-done = bf16[4096,384]{1,0:T(8,128)(2,1)} async-done(((bf16[128,384]{1,0:T(8,128)(2,1)}), bf16[4096,384]{1,0:T(8,128)(2,1)}) %all-gather.8.cloned.1.call-update) | async-done | bytes 3145744 | tf_op jit(solution)/shard_map/all_gather | solution.py:52
  257.5 3.8 %fusion.10 = f32[256,384]{1,0:T(8,128)S(1)} fusion(bf16[4096,256]{1,0:T(8,128)(2,1)} %bitcast.9, bf16[4096,384]{1,0:T(8,128)(2,1)} %all-gather.8.cloned.1.call-done), kind=kOutput, calls=%fused_computation.24 | convolution fusion | flops 805306368 | bytes 5636096 | tf_op jit(solution)/shard_map/dot_general | solution.py:50
  261.4 0.7 slice.28
  262.0 0.7 slice.29
  262.7 91.7 %reduce-scatter.2.cloned.1.call-done = bf16[8,8192]{1,0:T(8,128)(2,1)} async-done(((bf16[128,8192]{1,0:T(8,128)(2,1)}), bf16[8,8192]{1,0:T(8,128)(2,1)}) %reduce-scatter.2.cloned.1.call-update) | async-done | bytes 131088 | tf_op jit(solution)/shard_map/reduce_scatter | solution.py:41
  354.5 1.2 fusion.5
  355.6 1.7 fusion.8
  (7 shorter events, 0.0 us)
Async XLA Ops:
  7.2 73.8 %all-gather.6.cloned.1.call-start = ((), (), s32[]{:S(2)}) async-start(), calls=%async_computation.4 | async-start | bytes 2228224 | tf_op jit(solution)/shard_map/all_gather | solution.py:21
  7.9 178.7 %all-gather.4.cloned.1.call-start = ((), (), s32[]{:S(2)}) async-start(), calls=%async_computation.2 | async-start | bytes 6488064 | tf_op jit(solution)/shard_map/all_gather | solution.py:37
  9.6 247.9 %all-gather.8.cloned.1.call-start = ((), (), s32[]{:S(2)}) async-start(), calls=%async_computation.5 | async-start | bytes 3244032 | tf_op jit(solution)/shard_map/all_gather | solution.py:52
  9.6 8.5 %collective-permute-start = (bf16[128,256]{1,0:T(8,128)(2,1)}, bf16[128,256]{1,0:T(8,128)(2,1)S(1)}, u32[]{:S(2)}, u32[]{:S(2)}) collective-permute-start(bf16[128,256]{1,0:T(8,128)(2,1)} %bitcast.10), channel_id=1, source_target_pairs={{0,1},{1,0},{2,3},{3,2},{4,5},{5,4},{6,7},{7,6},{8,9},{9,8},{10,11... | collective-permute-start | bytes 196616 | tf_op jit(solution)/shard_map/ppermute | solution.py:8
  20.4 64.8 %copy-start.1 = (f32[8192]{0:T(1024)S(1)}, f32[8192]{0:T(1024)}, u32[]{:S(2)}) copy-start(f32[8192]{0:T(1024)} %param.7) | copy-start | bytes 98308
  89.7 96.9 %copy-start.2 = (bf16[128,256]{1,0:T(8,128)(2,1)S(1)}, bf16[128,256]{1,0:T(8,128)(2,1)}, u32[]{:S(2)}) copy-start(bf16[128,256]{1,0:T(8,128)(2,1)} %param.11) | copy-start | bytes 196612
  89.7 103.3 %all-to-all-start = ((bf16[128,32,256]{0,2,1:T(8,128)(2,1)}), bf16[128,32,256]{0,2,1:T(8,128)(2,1)S(1)}, u32[]{:S(2)}, u32[]{:S(2)}) async-start(bf16[128,32,256]{0,2,1:T(8,128)(2,1)} %bitcast.8), calls=%async_computation.1 | async-start | bytes 4194304 | tf_op jit(solution)/shard_map/all_to_all | solution.py:49
  98.4 94.3 %copy-start = (bf16[8,8192]{1,0:T(8,128)(2,1)S(1)}, bf16[8,8192]{1,0:T(8,128)(2,1)}, u32[]{:S(2)}) copy-start(bf16[8,8192]{1,0:T(8,128)(2,1)} %param.6) | copy-start | bytes 393220
  98.4 256.1 %reduce-scatter.2.cloned.1.call-start = ((), (), s32[]{:S(2)}) async-start(), calls=%async_computation.3 | async-start | bytes 2228224 | tf_op jit(solution)/shard_map/reduce_scatter | solution.py:41
Sparse Core Ops, SparseCore 0:
  11.0 69.8 all-gather.5
  83.7 102.8 all-gather.3
  189.3 68.1 all-gather.7
  261.5 92.9 reduce-scatter.1
where the time goes:
time: 365 us; the launch traced here: 364 us
  waiting for transfers between devices  305 us (84%)
  starting transfers between devices  15.5 us (4%)
  between operations  13.8 us (4%)
  other arithmetic  12.4 us (3%)
  matrix products  9.99 us (3%)
  local copies, waits for them, and re-layouts  7.55 us (2%)
    reduce_scatter x1, waiting for transfers between devices, on_device(): lax.psum_scatter(partials.astype(jnp.bfloat16), 'tensor', scatter_dimensi...  91.7 us
    all_gather x1, waiting for transfers between devices, on_device(): lax.all_gather(joint_weight, 'context', axis=0, tiled=True)  88.1 us
    all_gather x1, waiting for transfers between devices, on_device(): lax.all_gather(joint_grad, 'context', axis=0, tiled=True)  61.6 us
    all_gather x1, waiting for transfers between devices, on_device(): collected_rows = lax.all_gather(block_input, 'tensor', axis=0, tiled=True)  60.5 us
    all_to_all x1, starting transfers between devices, on_device(): lax.all_to_all(normalized_rows, 'context', split_axis=1, concat_axis=0, t...  8.71 us
  transfers between devices with their start and end apart: 6, of which 5 were waited for; matrix products, arithmetic and copies ran while one was open for 7% of the time, Pallas kernels for 0%

commit v1 on v0

v1 whole, which is shorter than its diff:
```python
import jax
import jax.numpy as jnp
from jax import lax
from jax.sharding import PartitionSpec as P


def partner_2(value, axis, bit):
    return lax.ppermute(value, axis, [(i, i ^ 1 << bit) for i in range(lax.axis_size(axis))])


def on_device(block_input, norm_scale_weight, kv_weight, q_weight, kv_cotangent, q_cotangent):
    n_context = lax.axis_size("context")
    n_tensor = lax.axis_size("tensor")
    own, features = block_input.shape
    depth = features // n_context
    rows32 = block_input.astype(jnp.float32)
    inv = lax.rsqrt(jnp.mean(rows32 * rows32, axis=-1, keepdims=True) + 1e-06)
    unit = rows32 * inv
    normed = (unit * norm_scale_weight).astype(jnp.bfloat16)
    spread = lax.all_to_all(
        normed.reshape(own, n_context, depth).transpose(1, 0, 2), "context", split_axis=0, concat_axis=0, tiled=True
    )
    gathered = lax.all_gather(spread, "tensor", axis=1)
    tokens = gathered.reshape(n_context * n_tensor * own, depth)
    width = kv_weight.shape[1]
    parity = lax.axis_index("tensor") % 2
    cotangent = kv_cotangent[:, 0, :]
    keys_part = cotangent[:, :width]
    values_part = cotangent[:, width:]
    mine = jnp.where(parity == 0, keys_part, values_part)
    other = partner_2(jnp.where(parity == 0, values_part, keys_part), "tensor", 0)
    head_grad = (mine.astype(jnp.float32) + other.astype(jnp.float32)).astype(jnp.bfloat16)
    joint_grad = jnp.concatenate([head_grad, q_cotangent], axis=1)
    joint_weight = jnp.concatenate([kv_weight, q_weight], axis=1)
    all_grad = lax.all_gather(joint_grad, "context", axis=0, tiled=True)
    partials = lax.dot_general(
        all_grad, joint_weight, (((1,), (1,)), ((), ())), preferred_element_type=jnp.float32
    ).astype(jnp.bfloat16)
    partials = partials.reshape(n_context, n_tensor, own, depth)
    summed = lax.psum_scatter(partials, "tensor", scatter_dimension=1, tiled=False)
    back = lax.all_to_all(summed, "context", split_axis=0, concat_axis=0, tiled=True)
    normed_grad = back.transpose(1, 0, 2).reshape(own, features).astype(jnp.float32)
    scaled = norm_scale_weight * normed_grad
    input_gradient = inv * (scaled - unit * jnp.mean(scaled * unit, axis=-1, keepdims=True))
    joint_result = lax.dot_general(
        tokens, all_grad, (((0,), (0,)), ((), ())), preferred_element_type=jnp.float32
    )
    return (input_gradient.astype(jnp.bfloat16), joint_result[:, :width], joint_result[:, width:])


def solution(mesh):
    in_specs = (
        P(("context", "tensor"), None),
        P(),
        P("context", "tensor"),
        P("context", "tensor"),
        P("context", "tensor", None),
        P("context", "tensor"),
    )
    out_specs = (P(("context", "tensor"), None), P("context", "tensor"), P("context", "tensor"))
    return jax.shard_map(
        on_device, mesh=mesh, in_specs=in_specs, out_specs=out_specs, check_vma=False
    )
```

time: 365 us -> 388 us (1.063)
  waiting for transfers between devices: 305 us -> 319 us
  blocking collectives: 0 us -> 13.3 us
  starting transfers between devices: 15.5 us -> 24.9 us
  other arithmetic: 12.4 us -> 4.33 us
    unnamed x4, waiting for transfers between devices: 0.73 us -> 174 us
    reduce_scatter x1 -> x0, waiting for transfers between devices: 91.7 us -> none  [on_device(): lax.psum_scatter(partials.astype(jnp.bfloat16), 'tensor', scatter_dimensi...]
    all_gather x3 -> x2, waiting for transfers between devices: 210 us -> 134 us  [the longest x1 73.9 us: on_device(): all_grad = lax.all_gather(joint_grad, 'context', axis=0, tiled=True)]
    all_to_all x0 -> x1, blocking collectives: none -> 13.3 us  [on_device(): lax.all_to_all(normed.reshape(own, n_context, depth).transpose(1, 0, 2),...]
    all_to_all x1, starting transfers between devices: 8.71 us -> 18.2 us  [on_device(): lax.all_to_all(summed, 'context', split_axis=0, concat_axis=0, tiled=True)]
    all_to_all x1, waiting for transfers between devices: 0.01 us -> 9.01 us  [on_device(): lax.all_to_all(summed, 'context', split_axis=0, concat_axis=0, tiled=True)]
    convert_element_type x3, other arithmetic: 6.87 us -> 1.6 us  [the longest x1 0.79 us: on_device(): (mine.astype(jnp.float32) + other.astype(jnp.float32)).astype(jnp.bfloat16)]
  transfers between devices with their start and end apart: 6 -> 5, of which waited for: 5 -> 5; matrix products, arithmetic and copies ran while one was open for 7% -> 0% of each run, Pallas kernels for 0% -> 0%
where the time goes in v1:
time: 388 us
  waiting for transfers between devices  319 us (82%)
  starting transfers between devices  24.9 us (6%)
  between operations  13.8 us (4%)
  blocking collectives  13.3 us (3%)
  matrix products  7.42 us (2%)
  local copies, waits for them, and re-layouts  5.03 us (1%)
  other arithmetic  4.33 us (1%)
    unnamed x4, waiting for transfers between devices  174 us
    all_gather x1, waiting for transfers between devices, on_device(): all_grad = lax.all_gather(joint_grad, 'context', axis=0, tiled=True)  73.9 us
    all_gather x1, waiting for transfers between devices, on_device(): gathered = lax.all_gather(spread, 'tensor', axis=1)  60.4 us
    all_to_all x1, starting transfers between devices, on_device(): lax.all_to_all(summed, 'context', split_axis=0, concat_axis=0, tiled=True)  18.2 us
    all_to_all x1, blocking collectives, on_device(): lax.all_to_all(normed.reshape(own, n_context, depth).transpose(1, 0, 2),...  13.3 us
    all_to_all x1, waiting for transfers between devices, on_device(): lax.all_to_all(summed, 'context', split_axis=0, concat_axis=0, tiled=True)  9.01 us
  transfers between devices with their start and end apart: 5, of which 5 were waited for; matrix products, arithmetic and copies ran while one was open for 0% of the time, Pallas kernels for 0%

profile of v1, /device:TPU:1, one launch (start us, length us, event | category | flops | bytes accessed | tf_op | source)
XLA Modules:
  0.0 387.9 jit_solution(17282549468111711338)
XLA Ops:
  7.2 0.0 all-gather.4.cloned.1.call-start
  7.2 0.8 broadcast_select_fusion
  8.0 6.6 %collective-permute-start = (bf16[128,128]{1,0:T(8,128)(2,1)S(1)}, bf16[128,128]{1,0:T(8,128)(2,1)S(1)}, u32[]{:S(2)}, u32[]{:S(2)}) collective-permute-start(bf16[128,128]{1,0:T(8,128)(2,1)S(1)} %broadcast_select_fusion), channel_id=1, source_target_pairs={{0,1},{1,0},{2,3},{3,2},{4,5},{5,4},{6,7},{7,6},{8,9},{9,8},{10,11... | collective-permute-start | bytes 98312 | tf_op jit(solution)/shard_map/ppermute | solution.py:8
  14.6 1.3 collective-permute-done
  15.9 0.8 add_convert_fusion
  16.7 1.5 pad_maximum_fusion
  18.2 0.0 all-gather.4.cloned.1.call-update
  18.2 0.0 copy-start.1
  18.3 0.0 all-reduce.3.cloned.1.call-start
  18.3 73.9 %all-gather.4.cloned.1.call-done = bf16[4096,384]{1,0:T(8,128)(2,1)} async-done(((bf16[128,384]{1,0:T(8,128)(2,1)}), bf16[4096,384]{1,0:T(8,128)(2,1)}) %all-gather.4.cloned.1.call-update) | async-done | bytes 3145744 | tf_op jit(solution)/shard_map/all_gather | solution.py:35
  92.2 4.5 %convolution_convert_fusion = bf16[4096,256]{1,0:T(8,128)(2,1)} fusion(bf16[4096,384]{1,0:T(8,128)(2,1)} %all-gather.4.cloned.1.call-done, bf16[256,256]{1,0:T(8,128)(2,1)} %param.9, bf16[256,128]{1,0:T(8,128)(2,1)} %param.8), kind=kOutput, calls=%fused_computation | convolution fusion | flops 806748160 | bytes 5439488 | tf_op jit(solution)/shard_map/dot_general | solution.py:36
  96.7 0.0 copy-start.2
  96.7 0.0 copy-start
  96.7 0.0 all-reduce.3.cloned.1.call-update
  96.8 1.4 dynamic-slice
  98.2 174.4 %all-reduce.3.cloned.1.call-done = bf16[32,16,8,256]{3,2,1,0:T(8,128)(2,1)} async-done(((bf16[32,16,8,256]{3,2,1,0:T(8,128)(2,1)}), bf16[32,16,8,256]{3,2,1,0:T(8,128)(2,1)}) %all-reduce.3.cloned.1.call-update) | async-done | bytes 2097168
  272.6 2.2 dynamic-slice_bitcast_fusion
  274.8 18.2 %all-to-all-start = ((bf16[32,8,256]{2,1,0:T(8,128)(2,1)}), bf16[32,8,256]{2,1,0:T(8,128)(2,1)S(1)}, u32[]{:S(2)}, u32[]{:S(2)}) async-start(bf16[32,8,256]{2,1,0:T(8,128)(2,1)} %dynamic-slice_bitcast_fusion), calls=%async_computation | async-start | bytes 262144 | tf_op jit(solution)/shard_map/all_to_all | solution.py:41
  293.0 0.0 all-gather.6.cloned.1.call-start
  293.0 0.0 copy-done.1
  293.0 0.2 fusion.8
  293.2 9.0 %all-to-all-done = bf16[32,8,256]{2,1,0:T(8,128)(2,1)S(1)} async-done(((bf16[32,8,256]{2,1,0:T(8,128)(2,1)}), bf16[32,8,256]{2,1,0:T(8,128)(2,1)S(1)}, u32[]{:S(2)}, u32[]{:S(2)}) %all-to-all-start) | async-done | bytes 131104 | tf_op jit(solution)/shard_map/all_to_all | solution.py:41
  302.2 0.0 copy-done.2
  302.2 0.3 fusion.3
  302.5 0.8 fusion.7
  303.3 13.3 %all_to_all.10 = bf16[32,8,256]{2,1,0:T(8,128)(2,1)} all-to-all(bf16[32,8,256]{2,1,0:T(8,128)(2,1)S(1)} %bitcast.20), channel_id=1, replica_groups=mesh['context'=32,'tensor'=16] {'context'}, dimensions={0} | all-to-all | bytes 262144 | tf_op jit(solution)/shard_map/all_to_all | solution.py:20
  316.6 0.0 all-gather.6.cloned.1.call-update
  316.7 60.4 %all-gather.6.cloned.1.call-done = bf16[32,128,256]{2,1,0:T(8,128)(2,1)} async-done(((bf16[32,8,256]{2,1,0:T(8,128)(2,1)}), bf16[32,128,256]{2,1,0:T(8,128)(2,1)}) %all-gather.6.cloned.1.call-update) | async-done | bytes 2097168 | tf_op jit(solution)/shard_map/all_gather | solution.py:23
  377.1 0.0 copy-done
  377.1 2.9 fusion.13
  380.0 0.7 slice.19
  380.7 0.7 slice.18
  (3 shorter events, 0.0 us)
Async XLA Ops:
  7.2 85.0 %all-gather.4.cloned.1.call-start = ((), (), s32[]{:S(2)}) async-start(), calls=%async_computation.2 | async-start | bytes 3244032 | tf_op jit(solution)/shard_map/all_gather | solution.py:35
  8.0 7.9 %collective-permute-start = (bf16[128,128]{1,0:T(8,128)(2,1)S(1)}, bf16[128,128]{1,0:T(8,128)(2,1)S(1)}, u32[]{:S(2)}, u32[]{:S(2)}) collective-permute-start(bf16[128,128]{1,0:T(8,128)(2,1)S(1)} %broadcast_select_fusion), channel_id=1, source_target_pairs={{0,1},{1,0},{2,3},{3,2},{4,5},{5,4},{6,7},{7,6},{8,9},{9,8},{10,11... | collective-permute-start | bytes 98312 | tf_op jit(solution)/shard_map/ppermute | solution.py:8
  18.2 274.8 %copy-start.1 = (bf16[8,8192]{1,0:T(8,128)(2,1)S(1)}, bf16[8,8192]{1,0:T(8,128)(2,1)}, u32[]{:S(2)}) copy-start(bf16[8,8192]{1,0:T(8,128)(2,1)} %param.6) | copy-start | bytes 393220
  18.3 254.3 %all-reduce.3.cloned.1.call-start = ((), (), s32[]{:S(2)}) async-start(), calls=%async_computation.4 | async-start | bytes 4194304
  96.7 205.5 %copy-start.2 = (f32[8192]{0:T(1024)S(1)}, f32[8192]{0:T(1024)}, u32[]{:S(2)}) copy-start(f32[8192]{0:T(1024)} %param.7) | copy-start | bytes 98308
  96.7 280.4 %copy-start = (bf16[4096,384]{1,0:T(8,128)(2,1)S(1)}, bf16[4096,384]{1,0:T(8,128)(2,1)}, u32[]{:S(2)}) copy-start(bf16[4096,384]{1,0:T(8,128)(2,1)} %all-gather.4.cloned.1.call-done) | copy-start | bytes 9437188
  274.8 27.4 %all-to-all-start = ((bf16[32,8,256]{2,1,0:T(8,128)(2,1)}), bf16[32,8,256]{2,1,0:T(8,128)(2,1)S(1)}, u32[]{:S(2)}, u32[]{:S(2)}) async-start(bf16[32,8,256]{2,1,0:T(8,128)(2,1)} %dynamic-slice_bitcast_fusion), calls=%async_computation | async-start | bytes 262144 | tf_op jit(solution)/shard_map/all_to_all | solution.py:41
  293.0 84.2 %all-gather.6.cloned.1.call-start = ((), (), s32[]{:S(2)}) async-start(), calls=%async_computation.3 | async-start | bytes 2228224 | tf_op jit(solution)/shard_map/all_gather | solution.py:23
Sparse Core Ops, SparseCore 0:
  18.4 73.8 all-gather.3
  96.9 175.6 all-reduce.2
  316.8 60.2 all-gather.5

commit v2 on v1

v2 whole, which is shorter than its diff:
```python
import jax
import jax.numpy as jnp
from jax import lax
from jax.experimental import pallas as pl
from jax.experimental.pallas import tpu as pltpu
from jax.sharding import PartitionSpec as P

NY, NZL, NK = 8, 2, 2
NX, NZH = 4, 4
F32, BF16 = jnp.float32, jnp.bfloat16
N_COPIES = 105


def kernel(
    x_ref, gain_ref, kvw_ref, qw_ref, kvc_ref, qc_ref,
    dx_ref, gkv_ref, gq_ref,
    xk_keep, xk_send, xk_recv, xb, xg, xt,
    wb, kv_send, kv_recv, gs, gb,
    pb, pr, fb, fr, fk_keep, fk_send, fk_recv,
    gwp, gw_own, gw1, gw2, gws,
    send_sems, recv_sems,
):
    context = lax.axis_index("context")
    tensor = lax.axis_index("tensor")
    y, zl, k = lax.div(context, NZL * NK), lax.rem(lax.div(context, NK), NZL), lax.rem(context, NK)
    x, zh = lax.div(tensor, NZH), lax.rem(tensor, NZH)
    ozl, ok = 1 - zl, 1 - k

    def at_y(step):
        return lax.rem(y + (step + NY) % NY, NY)

    def at_x(step):
        return lax.rem(x + (step + NX) % NX, NX)

    def at_zh(step):
        return lax.rem(zh + (step + NZH) % NZH, NZH)

    def dev(yy=y, zz=zl, kk=k, xx=x, hh=zh):
        return {"context": (yy * NZL + zz) * NK + kk, "tensor": xx * NZH + hh}

    zls = (zl, ozl)
    far = [(s, o) for s in range(NY) for o in range(2) if (s, o) != (0, 0)]
    core_peer = dev(kk=ok)
    right, left = dev(yy=at_y(1)), dev(yy=at_y(-1))

    names = {}
    pending = []

    def number(name):
        return names.setdefault(name, len(names))

    def send(name, src, dst, to):
        slot = number(name)
        pltpu.make_async_remote_copy(
            src_ref=src, dst_ref=dst, send_sem=send_sems.at[slot], recv_sem=recv_sems.at[slot],
            device_id=to, device_id_type=pl.DeviceIdType.MESH,
        ).start()
        pending.append((src, slot))

    def arrived(name, dst):
        pltpu.make_async_copy(dst, dst, recv_sems.at[number(name)]).wait()

    peers = [core_peer]
    peers += [dev(yy=at_y(s), zz=zls[o]) for s, o in far]
    peers += [dev(xx=at_x(s)) for s in range(1, NX)]
    peers += [dev(hh=at_zh(s)) for s in range(1, NZH)]
    barrier = pltpu.get_barrier_semaphore()
    for peer in peers:
        pl.semaphore_signal(barrier, inc=1, device_id=peer, device_id_type=pl.DeviceIdType.MESH)

    parity = lax.rem(zh, 2)
    kvc = kvc_ref[...].astype(F32)
    keys, values = kvc[:, :128], kvc[:, 128:]
    kv_send[...] = jnp.where(parity == 0, values, keys).astype(BF16)
    pl.semaphore_wait(barrier, len(peers))

    send("kv", kv_send, kv_recv, dev(hh=zh + 1 - 2 * parity))

    rows = x_ref[...].astype(F32)
    inv = lax.rsqrt(jnp.mean(rows * rows, axis=-1, keepdims=True) + 1e-06)
    for b in range(NY * NZL):
        both = []
        for j in (0, 1):
            cols = slice((2 * b + j) * 256, (2 * b + j + 1) * 256)
            both.append((rows[:, cols] * inv * gain_ref[:, cols]).astype(BF16).astype(F32))
        xk_keep[b] = jnp.where(k == 0, both[0], both[1])
        xk_send[b] = jnp.where(k == 0, both[1], both[0])
    send("xk", xk_send, xk_recv, core_peer)

    arrived("kv", kv_recv)
    head = (jnp.where(parity == 0, keys, values) + kv_recv[...].astype(F32)).astype(BF16)
    for j in range(NX):
        gs[j, :, :128] = head[32 * j:32 * j + 32]
        gs[j, :, 128:] = qc_ref[32 * j:32 * j + 32, :]
    for s in (2, 1, 3):
        send(("ga", s), gs.at[at_x(s)], gb.at[y, k, zl, x], dev(xx=at_x(s)))
    gb[y, k, zl, x] = gs[x]

    wb[x, :, :128] = kvw_ref[...]
    wb[x, :, 128:] = qw_ref[...]
    send("w_right", wb.at[x], wb.at[x], dev(xx=at_x(1)))
    send("w_left", wb.at[x], wb.at[x], dev(xx=at_x(-1)))

    arrived("xk", xk_recv)
    for b in range(NY * NZL):
        keep, recv = xk_keep[b], xk_recv[b]
        pair = [jnp.where(k == 0, keep, recv), jnp.where(k == 0, recv, keep)]
        xb[b] = jnp.concatenate(pair, axis=0).astype(BF16)
    for s, o in far:
        send(("xa", s, o), xb.at[at_y(s) * NZL + zls[o]], xg.at[zh, y, zl], dev(yy=at_y(s), zz=zls[o]))
    xg[zh, y, zl] = xb[y * NZL + zl]

    for s in (1, 2, 3):
        arrived(("ga", s), gb.at[y, k, zl, at_x(-s)])

    def block(step, o):
        return gb.at[at_y(step), k, zls[o]]

    def ring_right(hop, o):
        send(("gr", hop, o), block(1 - hop, o), block(1 - hop, o), right)

    def ring_left(hop, o):
        send(("gl", hop, o), block(hop - 1, o), block(hop - 1, o), left)

    def to_core(step, o):
        send(("gk", step, o), block(step, o), block(step, o), core_peer)

    ring_right(1, 0)
    ring_left(1, 0)
    send("gz", block(0, 0), block(0, 0), dev(zz=ozl))
    to_core(0, 0)

    def normed_grad_terms(step):
        yy = at_y(step)
        for o in (0, 1):
            arrived(("gk", step, o), gb.at[yy, ok, zls[o]])
        acc = jnp.zeros((128, 256), F32)
        for j in range(NX):
            acc += lax.dot_general(
                gb[yy, :, :, j].reshape(128, 384), wb[j], (((1,), (1,)), ((), ())), preferred_element_type=F32
            )
        for h in range(NZH):
            for z in range(NZL):
                start = z * 32 + h * 8
                pb[yy, h, z] = jnp.concatenate([acc[start:start + 8], acc[64 + start:72 + start]], axis=0).astype(BF16)
        for s in (2, 1, 3):
            send(("p", step, s), pb.at[yy, at_zh(s)], pr.at[yy, zh], dev(hh=at_zh(s)))

    def normed_grad_sum(step):
        yy = at_y(step)
        for s in (1, 2, 3):
            arrived(("p", step, s), pr.at[yy, at_zh(-s)])
        total = pb[yy, zh].astype(F32)
        for s in (1, 2, 3):
            total += pr[yy, at_zh(s)].astype(F32)
        fb[yy] = total.astype(BF16)
        for o in (0, 1):
            if (step, o) != (0, 0):
                send(("f", step % NY, o), fb.at[yy, zls[o]], fr.at[y, zl], dev(yy=yy, zz=zls[o]))
        if step == 0:
            fr[y, zl] = fb[y, zl]

    arrived("gz", block(0, 1))
    ring_right(1, 1)
    ring_left(1, 1)
    to_core(0, 1)

    for s, o in far:
        arrived(("xa", s, o), xg.at[zh, at_y(-s), zls[o]])
    send("x_right", xg.at[zh], xg.at[zh], dev(hh=at_zh(1)))
    send("x_left", xg.at[zh], xg.at[zh], dev(hh=at_zh(-1)))

    arrived("w_right", wb.at[at_x(-1)])
    part = wb.at[at_x(-1), pl.ds(0, 128)]
    send("w_far0", part, part, dev(xx=at_x(1)))
    arrived("w_left", wb.at[at_x(1)])
    part = wb.at[at_x(1), pl.ds(128, 128)]
    send("w_far1", part, part, dev(xx=at_x(-1)))

    def hop_arrivals(hop):
        for o in (0, 1):
            if hop < 4 or o == 0:
                arrived(("gr", hop, o), block(-hop, o))
                if hop + 1 < 4 or (hop + 1 == 4 and o == 0):
                    ring_right(hop + 1, o)
                to_core(-hop if hop < 4 else 4, o)
            if hop < 4 or o == 1:
                arrived(("gl", hop, o), block(hop, o))
                if hop + 1 < 4 or (hop + 1 == 4 and o == 1):
                    ring_left(hop + 1, o)
                to_core(hop, o)

    hop_arrivals(1)

    arrived("x_right", xg.at[at_zh(-1)])
    part = xg.at[at_zh(-1), pl.ds(0, 4)]
    send("x_far0", part, part, dev(hh=at_zh(1)))
    arrived("x_left", xg.at[at_zh(1)])
    part = xg.at[at_zh(1), pl.ds(4, 4)]
    send("x_far1", part, part, dev(hh=at_zh(-1)))
    arrived("w_far0", wb.at[at_x(2), pl.ds(0, 128)])
    arrived("w_far1", wb.at[at_x(2), pl.ds(128, 128)])
    normed_grad_terms(0)

    hop_arrivals(2)
    normed_grad_terms(-1)
    normed_grad_terms(1)
    normed_grad_sum(0)

    arrived("x_far0", xg.at[at_zh(2), pl.ds(0, 4)])
    arrived("x_far1", xg.at[at_zh(2), pl.ds(4, 4)])

    def turn(yy, carry):
        tiles = [[xg[h, yy, z].astype(F32) for z in range(NZL)] for h in range(NZH)]
        order = [tiles[h][z][8 * c:8 * c + 8] for c in range(NK) for z in range(NZL) for h in range(NZH)]
        xt[:, pl.ds(pl.multiple_of(yy * 128, 128), 128)] = jnp.concatenate(order, axis=0).T.astype(BF16)
        return carry

    lax.fori_loop(0, NY, turn, 0)

    hop_arrivals(3)
    normed_grad_terms(-2)
    normed_grad_terms(2)
    normed_grad_sum(-1)
    normed_grad_sum(1)
    hop_arrivals(4)
    normed_grad_terms(-3)
    normed_grad_terms(3)
    normed_grad_sum(-2)
    normed_grad_sum(2)
    normed_grad_terms(4)

    def weight_grad(xx):
        g = gb[:, :, :, xx].reshape(1024, 384)
        return jnp.dot(xt[...], g, preferred_element_type=F32)

    x1, x2, x3 = at_x(1), at_x(2), at_x(3)
    gwp[x2] = weight_grad(x2).astype(BF16)
    send("gw_a", gwp.at[x2, pl.ds(0, 128)], gw1.at[0], dev(xx=x1))
    send("gw_b", gwp.at[x2, pl.ds(128, 128)], gw1.at[1], dev(xx=x3))
    gwp[x1] = weight_grad(x1).astype(BF16)
    send("gw_c", gwp.at[x1, pl.ds(128, 128)], gw2.at[0, 1], dev(xx=x1))
    gwp[x3] = weight_grad(x3).astype(BF16)
    send("gw_d", gwp.at[x3, pl.ds(0, 128)], gw2.at[1, 0], dev(xx=x3))
    normed_grad_sum(-3)
    normed_grad_sum(3)
    normed_grad_sum(4)
    arrived("gw_a", gw1.at[0])
    gws[0] = (gwp[x1, 0:128].astype(F32) + gw1[0].astype(F32)).astype(BF16)
    send("gw_e", gws.at[0], gw2.at[0, 0], dev(xx=x1))
    arrived("gw_b", gw1.at[1])
    gws[1] = (gwp[x3, 128:256].astype(F32) + gw1[1].astype(F32)).astype(BF16)
    send("gw_f", gws.at[1], gw2.at[1, 1], dev(xx=x3))
    gw_own[...] = weight_grad(x)

    for s, o in far:
        arrived(("f", s, o), fr.at[at_y(-s), zls[o]])
    for b in range(NY * NZL):
        tile = fr[b // NZL, b % NZL].astype(F32)
        fk_keep[b] = jnp.where(k == 0, tile[:8], tile[8:])
        fk_send[b] = jnp.where(k == 0, tile[8:], tile[:8])
    send("fk", fk_send, fk_recv, core_peer)
    arrived("fk", fk_recv)
    rows = x_ref[...].astype(F32)
    inv = lax.rsqrt(jnp.mean(rows * rows, axis=-1, keepdims=True) + 1e-06)
    dot = jnp.zeros((8, 256), F32)
    blocks = []
    for b in range(NY * NZL):
        keep, recv = fk_keep[b], fk_recv[b]
        for j, part in enumerate([jnp.where(k == 0, keep, recv), jnp.where(k == 0, recv, keep)]):
            cols = slice((2 * b + j) * 256, (2 * b + j + 1) * 256)
            dot += (part * gain_ref[:, cols]) * (rows[:, cols] * inv)
            blocks.append((part, cols))
    mean = jnp.sum(dot, axis=-1, keepdims=True) * (1.0 / (256 * len(blocks)))
    for part, cols in blocks:
        dx_ref[:, cols] = (inv * (part * gain_ref[:, cols] - rows[:, cols] * inv * mean)).astype(BF16)

    arrived("gw_c", gw2.at[0, 1])
    arrived("gw_d", gw2.at[1, 0])
    arrived("gw_e", gw2.at[0, 0])
    arrived("gw_f", gw2.at[1, 1])
    for half in (0, 1):
        at = slice(128 * half, 128 * half + 128)
        total = gw_own[at] + gw2[0, half].astype(F32) + gw2[1, half].astype(F32)
        gkv_ref[at] = total[:, :128]
        gq_ref[at] = total[:, 128:]
    for src, slot in pending:
        pltpu.make_async_copy(src, src, send_sems.at[slot]).wait()
    assert len(names) == N_COPIES, len(names)


def on_device(block_input, norm_scale_weight, kv_weight, q_weight, kv_cotangent, q_cotangent):
    vmem = pl.BlockSpec(memory_space=pltpu.VMEM)

    def buf(dtype, *shape):
        return pltpu.VMEM(shape, dtype)

    return pl.pallas_call(
        kernel,
        out_shape=(
            jax.ShapeDtypeStruct((8, 8192), BF16),
            jax.ShapeDtypeStruct((256, 128), F32),
            jax.ShapeDtypeStruct((256, 256), F32),
        ),
        in_specs=[vmem] * 6,
        out_specs=(vmem,) * 3,
        scratch_shapes=[
            buf(F32, 16, 8, 256), buf(F32, 16, 8, 256), buf(F32, 16, 8, 256),
            buf(BF16, 16, 16, 256), buf(BF16, 4, 8, 2, 16, 256), buf(BF16, 256, 1024),
            buf(BF16, 4, 256, 384), buf(BF16, 128, 128), buf(BF16, 128, 128),
            buf(BF16, 4, 32, 384), buf(BF16, 8, 2, 2, 4, 32, 384),
            buf(BF16, 8, 4, 2, 16, 256), buf(BF16, 8, 4, 2, 16, 256),
            buf(BF16, 8, 2, 16, 256), buf(BF16, 8, 2, 16, 256),
            buf(F32, 16, 8, 256), buf(F32, 16, 8, 256), buf(F32, 16, 8, 256),
            buf(BF16, 4, 256, 384), buf(F32, 256, 384), buf(BF16, 2, 128, 384),
            buf(BF16, 2, 2, 128, 384), buf(BF16, 2, 128, 384),
            pltpu.SemaphoreType.DMA((N_COPIES,)), pltpu.SemaphoreType.DMA((N_COPIES,)),
        ],
        compiler_params=pltpu.CompilerParams(
            collective_id=0, has_side_effects=True, vmem_limit_bytes=40 * 1024 * 1024
        ),
        cost_estimate=pl.CostEstimate(flops=1_700_000_000, bytes_accessed=2_000_000, transcendentals=16),
        name="qkv_backward",
    )(
        block_input, norm_scale_weight.reshape(1, -1), kv_weight, q_weight,
        kv_cotangent.reshape(kv_cotangent.shape[0], -1), q_cotangent,
    )


def solution(mesh):
    in_specs = (
        P(("context", "tensor"), None),
        P(),
        P("context", "tensor"),
        P("context", "tensor"),
        P("context", "tensor", None),
        P("context", "tensor"),
    )
    out_specs = (P(("context", "tensor"), None), P("context", "tensor"), P("context", "tensor"))
    return jax.shard_map(
        on_device, mesh=mesh, in_specs=in_specs, out_specs=out_specs, check_vma=False
    )
```

time: 388 us -> 72.9 us (0.19)
  waiting for transfers between devices: 319 us -> 0 us
  Pallas kernels: 0 us -> 64.8 us
  starting transfers between devices: 24.9 us -> 0 us
  blocking collectives: 13.3 us -> 0 us
  between operations: 13.8 us -> 0.65 us
  matrix products: 7.42 us -> 0 us
  other arithmetic: 4.33 us -> 0 us
    unnamed x4 -> x0, waiting for transfers between devices: 174 us -> none
    all_gather x2 -> x0, waiting for transfers between devices: 134 us -> none  [the longest x1 73.9 us: on_device(): all_grad = lax.all_gather(joint_grad, 'context', axis=0, tiled=True)]
    pallas_call x0 -> x1, Pallas kernels: none -> 64.8 us  [on_device(): pl.pallas_call(kernel, out_shape=(jax.ShapeDtypeStruct((8, 8192), BF16),...]
    all_to_all x1 -> x0, starting transfers between devices: 18.2 us -> none  [on_device(): lax.all_to_all(summed, 'context', split_axis=0, concat_axis=0, tiled=True)]
    all_to_all x1 -> x0, blocking collectives: 13.3 us -> none  [on_device(): lax.all_to_all(normed.reshape(own, n_context, depth).transpose(1, 0, 2),...]
    all_to_all x1 -> x0, waiting for transfers between devices: 9.01 us -> none  [on_device(): lax.all_to_all(summed, 'context', split_axis=0, concat_axis=0, tiled=True)]
    dot_general x2 -> x0, matrix products: 7.42 us -> none  [the longest x1 4.53 us: on_device(): lax.dot_general(all_grad, joint_weight, (((1,), (1,)), ((), ())), preferr...]
    ppermute x1 -> x0, starting transfers between devices: 6.63 us -> none  [partner_2(): lax.ppermute(value, axis, [(i, i ^ 1 << bit) for i in range(lax.axis_size...]
  transfers between devices with their start and end apart: 5 -> 0, of which waited for: 5 -> 0; matrix products, arithmetic and copies ran while one was open for 0% -> 0% of each run, Pallas kernels for 0% -> 0%
where the time goes in v2:
time: 72.9 us; the launch traced here: 72.5 us
  Pallas kernels  64.8 us (89%)
  local copies, waits for them, and re-layouts  7.09 us (10%)
    pallas_call x1, Pallas kernels, on_device(): pl.pallas_call(kernel, out_shape=(jax.ShapeDtypeStruct((8, 8192), BF16),...  64.8 us
    unnamed x15, local copies, waits for them, and re-layouts  7.09 us

profile of v2, /device:TPU:1, one launch (start us, length us, event | category | flops | bytes accessed | tf_op | source)
XLA Modules:
  0.0 72.5 jit_solution(4883459971447496818)
XLA Ops:
  0.6 0.0 copy-start
  0.6 0.9 %copy-done = bf16[8,8192]{1,0:T(8,128)(2,1)S(1)} copy-done((bf16[8,8192]{1,0:T(8,128)(2,1)S(1)}, bf16[8,8192]{1,0:T(8,128)(2,1)}, u32[]{:S(2)}) %copy-start) | copy-done | bytes 131096
  1.5 0.0 copy-start.1
  1.5 0.9 %copy-done.1 = bf16[256,256]{1,0:T(8,128)(2,1)S(1)} copy-done((bf16[256,256]{1,0:T(8,128)(2,1)S(1)}, bf16[256,256]{1,0:T(8,128)(2,1)}, u32[]{:S(2)}) %copy-start.1) | copy-done | bytes 131096
  2.4 0.0 copy-start.2
  2.4 0.8 %copy-done.2 = bf16[256,128]{1,0:T(8,128)(2,1)S(1)} copy-done((bf16[256,128]{1,0:T(8,128)(2,1)S(1)}, bf16[256,128]{1,0:T(8,128)(2,1)}, u32[]{:S(2)}) %copy-start.2) | copy-done | bytes 65560
  3.3 0.0 copy-start.3
  3.3 0.8 %copy-done.3 = bf16[128,1,256]{2,0,1:T(8,128)(2,1)S(1)} copy-done((bf16[128,1,256]{2,0,1:T(8,128)(2,1)S(1)}, bf16[128,1,256]{2,0,1:T(8,128)(2,1)}, u32[]{:S(2)}) %copy-start.3) | copy-done | bytes 65560
  4.1 0.0 copy-start.4
  4.1 0.8 %copy-done.4 = bf16[128,256]{1,0:T(8,128)(2,1)S(1)} copy-done((bf16[128,256]{1,0:T(8,128)(2,1)S(1)}, bf16[128,256]{1,0:T(8,128)(2,1)}, u32[]{:S(2)}) %copy-start.4) | copy-done | bytes 65560
  5.0 0.0 copy-start.5
  5.0 0.8 %copy-done.5 = f32[8192]{0:T(1024)S(1)} copy-done((f32[8192]{0:T(1024)S(1)}, f32[8192]{0:T(1024)}, u32[]{:S(2)}) %copy-start.5) | copy-done | bytes 32792
  5.7 64.8 %qkv_backward.1 = (bf16[8,8192]{1,0:T(8,128)(2,1)S(1)}, f32[256,128]{1,0:T(8,128)S(1)}, f32[256,256]{1,0:T(8,128)S(1)}) custom-call(bf16[8,8192]{1,0:T(8,128)(2,1)S(1)} %copy-done, f32[1,8192]{1,0:T(1,128)S(1)} %bitcast.3, bf16[256,128]{1,0:T(8,128)(2,1)S(1)} %copy-done.2, bf16[256,256]{1,0:T(8,128)(2,1)S(1)} %copy-done.1, bf16[128,256]{1,0:T(8,128)(2,1)S(1)} %bitcast.2, ...), custom_call_target="tpu_custom_call" | custom-call | flops 1700000000 | bytes 2000000 | tf_op jit(solution)/shard_map/qkv_backward/pallas_call | solution.py:298
  70.5 0.7 copy.12
  71.1 0.7 copy.13
  71.8 0.7 copy.14
Async XLA Ops:
  0.6 0.9 %copy-start = (bf16[8,8192]{1,0:T(8,128)(2,1)S(1)}, bf16[8,8192]{1,0:T(8,128)(2,1)}, u32[]{:S(2)}) copy-start(bf16[8,8192]{1,0:T(8,128)(2,1)} %x_ref.1) | copy-start | bytes 393220
  1.5 0.9 %copy-start.1 = (bf16[256,256]{1,0:T(8,128)(2,1)S(1)}, bf16[256,256]{1,0:T(8,128)(2,1)}, u32[]{:S(2)}) copy-start(bf16[256,256]{1,0:T(8,128)(2,1)} %qw_ref.1) | copy-start | bytes 393220
  2.4 0.8 %copy-start.2 = (bf16[256,128]{1,0:T(8,128)(2,1)S(1)}, bf16[256,128]{1,0:T(8,128)(2,1)}, u32[]{:S(2)}) copy-start(bf16[256,128]{1,0:T(8,128)(2,1)} %kvw_ref.1) | copy-start | bytes 196612
  3.3 0.8 %copy-start.3 = (bf16[128,1,256]{2,0,1:T(8,128)(2,1)S(1)}, bf16[128,1,256]{2,0,1:T(8,128)(2,1)}, u32[]{:S(2)}) copy-start(bf16[128,1,256]{2,0,1:T(8,128)(2,1)} %param.10) | copy-start | bytes 196612
  4.1 0.8 %copy-start.4 = (bf16[128,256]{1,0:T(8,128)(2,1)S(1)}, bf16[128,256]{1,0:T(8,128)(2,1)}, u32[]{:S(2)}) copy-start(bf16[128,256]{1,0:T(8,128)(2,1)} %qc_ref.1) | copy-start | bytes 196612
  5.0 0.8 %copy-start.5 = (f32[8192]{0:T(1024)S(1)}, f32[8192]{0:T(1024)}, u32[]{:S(2)}) copy-start(f32[8192]{0:T(1024)} %param.7) | copy-start | bytes 98308

commit v3 on v2

v3 whole, which is shorter than its diff:
```python
import jax
import jax.numpy as jnp
from jax import lax
from jax.experimental import pallas as pl
from jax.experimental.pallas import tpu as pltpu
from jax.sharding import PartitionSpec as P

NY, NZL, NK = 8, 2, 2
NX, NZH = 4, 4
F32, BF16 = jnp.float32, jnp.bfloat16
N_SEND, N_RECV = 29, 153
VL = 63_400_000


def kernel(
    x_hbm, gain_hbm, kvw_hbm, qw_hbm, kvc_hbm, qc_hbm,
    dx_ref, gkv_ref, gq_ref,
    x_ref, gain_ref, kvw_ref, qw_ref, kvc_ref, qc_ref, unit_ref,
    xk_keep, xk_send, xk_recv, xb, xg, xt,
    wb, ks, kb, gs, gb,
    pb, pr, fb, fr, fk_keep, fk_send, fk_recv,
    gwp, gw_own, gw1, gw2, gws,
    load_sems, send_sems, recv_sems,
):
    loads = [
        pltpu.make_async_copy(src, dst, load_sems.at[i])
        for i, (src, dst) in enumerate([
            (x_hbm, x_ref), (gain_hbm, gain_ref), (kvc_hbm, kvc_ref),
            (qc_hbm, qc_ref), (kvw_hbm, kvw_ref), (qw_hbm, qw_ref),
        ])
    ]
    for load in loads:
        load.start()

    context = lax.axis_index("context")
    tensor = lax.axis_index("tensor")
    y, zl, k = lax.div(context, NZL * NK), lax.rem(lax.div(context, NK), NZL), lax.rem(context, NK)
    x, zh = lax.div(tensor, NZH), lax.rem(tensor, NZH)
    ozl, ok = 1 - zl, 1 - k
    parity = lax.rem(zh, 2)
    ozh = zh + 1 - 2 * parity

    def at_y(step):
        return lax.rem(y + (step + NY) % NY, NY)

    def at_x(step):
        return lax.rem(x + (step + NX) % NX, NX)

    def at_zh(step):
        return lax.rem(zh + (step + NZH) % NZH, NZH)

    def dev(yy=y, zz=zl, kk=k, xx=x, hh=zh):
        return {"context": (yy * NZL + zz) * NK + kk, "tensor": xx * NZH + hh}

    zls = (zl, ozl)
    far = [(s, o) for s in range(NY) for o in range(2) if (s, o) != (0, 0)]
    core_peer = dev(kk=ok)
    right, left = dev(yy=at_y(1)), dev(yy=at_y(-1))

    recv_names, send_names = {}, {}

    def send(name, src, dst, to, group=None):
        slot = recv_names.setdefault(name, len(recv_names))
        group = name if group is None else group
        sent = send_names.setdefault(group, len(send_names))
        pltpu.make_async_remote_copy(
            src_ref=src, dst_ref=dst, send_sem=send_sems.at[sent], recv_sem=recv_sems.at[slot],
            device_id=to, device_id_type=pl.DeviceIdType.MESH,
        ).start()
        pending.setdefault(group, src)

    def arrived(name, dst):
        slot = recv_names.setdefault(name, len(recv_names))
        pltpu.make_async_copy(dst, dst, recv_sems.at[slot]).wait()

    pending = {}

    def drain():
        for group, src in pending.items():
            pltpu.make_async_copy(src, src, send_sems.at[send_names[group]]).wait()
        pending.clear()

    peers = [dev(yy=at_y(s), zz=zls[o]) for s, o in far]
    peers += [dev(hh=at_zh(s)) for s in range(1, NZH)]
    peers += [dev(xx=at_x(s)) for s in range(1, NX)]
    peers += [dev(xx=at_x(s), hh=ozh) for s in range(1, NX)]
    peers += [core_peer]
    barrier = pltpu.get_barrier_semaphore()
    for peer in peers:
        pl.semaphore_signal(barrier, inc=1, device_id=peer, device_id_type=pl.DeviceIdType.MESH)

    loads[2].wait()
    loads[3].wait()
    for j in range(NX):
        part = kvc_ref[32 * j:32 * j + 32, :]
        keys, values = part[:, :128], part[:, 128:]
        gs[j, :, :128] = jnp.where(parity == 0, keys, values)
        gs[j, :, 128:] = qc_ref[32 * j:32 * j + 32, :]
        ks[j] = jnp.where(parity == 0, values, keys)
    pl.semaphore_wait(barrier, len(peers))
    send(("kb", 0), ks.at[x], kb.at[x], dev(hh=ozh))
    for s in (2, 1, 3):
        send(("kb", s), ks.at[at_x(s)], kb.at[x], dev(xx=at_x(s), hh=ozh))
        send(("ga", s), gs.at[at_x(s)], gb.at[y, k, zl, x], dev(xx=at_x(s)))
    gb[y, k, zl, x] = gs[x]

    loads[0].wait()
    loads[1].wait()
    rows = x_ref[...].astype(F32)
    inv = lax.rsqrt(jnp.mean(rows * rows, axis=-1, keepdims=True) + 1e-06)
    for b in range(NY * NZL):
        both = []
        for j in (0, 1):
            cols = slice((2 * b + j) * 256, (2 * b + j + 1) * 256)
            unit = rows[:, cols] * inv
            unit_ref[:, cols] = unit
            both.append((unit * gain_ref[:, cols]).astype(BF16).astype(F32))
        xk_keep[b] = jnp.where(k == 0, both[0], both[1])
        xk_send[b] = jnp.where(k == 0, both[1], both[0])
    send("xk", xk_send, xk_recv, core_peer)

    loads[4].wait()
    loads[5].wait()
    wb[x, :, :128] = kvw_ref[...]
    wb[x, :, 128:] = qw_ref[...]
    send("w_right", wb.at[x], wb.at[x], dev(xx=at_x(1)))
    send("w_left", wb.at[x], wb.at[x], dev(xx=at_x(-1)))

    arrived("xk", xk_recv)
    for b in range(NY * NZL):
        keep, recv = xk_keep[b], xk_recv[b]
        pair = [jnp.where(k == 0, keep, recv), jnp.where(k == 0, recv, keep)]
        xb[b] = jnp.concatenate(pair, axis=0).astype(BF16)
    for s, o in far:
        send(("xa", s, o), xb.at[at_y(s) * NZL + zls[o]], xg.at[zh, y, zl], dev(yy=at_y(s), zz=zls[o]), "xa")
    pending["xa"] = xb.at[pl.ds(0, 15)]
    xg[zh, y, zl] = xb[y * NZL + zl]

    def block(step, o):
        return gb.at[at_y(step), k, zls[o]]

    def ring(hop, o, s):
        piece = at_x(-s)
        if hop < 4 or (hop == 4 and o == 0):
            at = block(1 - hop, o).at[piece]
            send(("gr", hop, o, s), at, at, right, "ring")
        if hop < 4 or (hop == 4 and o == 1):
            at = block(hop - 1, o).at[piece]
            send(("gl", hop, o, s), at, at, left, "ring")

    def to_core(step, o):
        send(("gk", step, o), block(step, o), block(step, o), core_peer, "gk")

    pieces = (0, 1, 3, 2)
    for s in pieces:
        piece = at_x(-s)
        arrived(("kb", s), kb.at[piece])
        if s:
            arrived(("ga", s), gb.at[y, k, zl, piece])
        head = gb[y, k, zl, piece, :, :128].astype(F32) + kb[piece].astype(F32)
        gb[y, k, zl, piece, :, :128] = head.astype(BF16)
        ring(1, 0, s)
        at = block(0, 0).at[piece]
        send(("gz", s), at, at, dev(zz=ozl), "gz")
    pending["gz"] = block(0, 0)
    to_core(0, 0)

    def hop_arrivals(hop, o):
        if hop == 0:
            for s in pieces:
                arrived(("gz", s), block(0, 1).at[at_x(-s)])
                ring(1, 1, s)
            to_core(0, 1)
            return
        for s in pieces:
            if hop < 4 or o == 0:
                arrived(("gr", hop, o, s), block(-hop, o).at[at_x(-s)])
            if hop < 4 or o == 1:
                arrived(("gl", hop, o, s), block(hop, o).at[at_x(-s)])
            ring(hop + 1, o, s)
        if hop < 4:
            to_core(-hop, o)
        to_core(hop, o)

    def normed_grad_terms(step):
        yy = at_y(step)
        for o in (0, 1):
            arrived(("gk", step, o), gb.at[yy, ok, zls[o]])
        acc = jnp.zeros((128, 256), F32)
        for j in range(NX):
            acc += lax.dot_general(
                gb[yy, :, :, j].reshape(128, 384), wb[j], (((1,), (1,)), ((), ())), preferred_element_type=F32
            )
        for h in range(NZH):
            for z in range(NZL):
                start = z * 32 + h * 8
                pb[yy, h, z] = jnp.concatenate([acc[start:start + 8], acc[64 + start:72 + start]], axis=0).astype(BF16)
        for s in (2, 1, 3):
            send(("p", step, s), pb.at[yy, at_zh(s)], pr.at[yy, zh], dev(hh=at_zh(s)), "p")

    def normed_grad_sum(step):
        yy = at_y(step)
        for s in (1, 3, 2):
            arrived(("p", step, s), pr.at[yy, at_zh(-s)])
        total = pb[yy, zh].astype(F32)
        for s in (1, 2, 3):
            total += pr[yy, at_zh(s)].astype(F32)
        fb[yy] = total.astype(BF16)
        for o in (0, 1):
            if (step, o) != (0, 0):
                send(("f", step % NY, o), fb.at[yy, zls[o]], fr.at[y, zl], dev(yy=yy, zz=zls[o]), "f")
        if step == 0:
            fr[y, zl] = fb[y, zl]

    hop_arrivals(1, 0)
    hop_arrivals(0, 1)

    for s, o in far:
        arrived(("xa", s, o), xg.at[zh, at_y(-s), zls[o]])
    send("x_right", xg.at[zh], xg.at[zh], dev(hh=at_zh(1)))
    send("x_left", xg.at[zh], xg.at[zh], dev(hh=at_zh(-1)))

    arrived("w_right", wb.at[at_x(-1)])
    part = wb.at[at_x(-1), pl.ds(0, 128)]
    send("w_far0", part, part, dev(xx=at_x(1)))
    arrived("w_left", wb.at[at_x(1)])
    part = wb.at[at_x(1), pl.ds(128, 128)]
    send("w_far1", part, part, dev(xx=at_x(-1)))

    hop_arrivals(2, 0)
    hop_arrivals(1, 1)

    arrived("x_right", xg.at[at_zh(-1)])
    part = xg.at[at_zh(-1), pl.ds(0, 4)]
    send("x_far0", part, part, dev(hh=at_zh(1)))
    arrived("x_left", xg.at[at_zh(1)])
    part = xg.at[at_zh(1), pl.ds(4, 4)]
    send("x_far1", part, part, dev(hh=at_zh(-1)))
    arrived("w_far0", wb.at[at_x(2), pl.ds(0, 128)])
    arrived("w_far1", wb.at[at_x(2), pl.ds(128, 128)])
    normed_grad_terms(0)

    hop_arrivals(3, 0)
    normed_grad_terms(-1)
    normed_grad_terms(1)
    hop_arrivals(2, 1)
    hop_arrivals(4, 0)
    normed_grad_terms(-2)
    normed_grad_terms(2)
    hop_arrivals(3, 1)

    arrived("x_far0", xg.at[at_zh(2), pl.ds(0, 4)])
    arrived("x_far1", xg.at[at_zh(2), pl.ds(4, 4)])

    def turn(yy, carry):
        tiles = [[xg[h, yy, z].astype(F32) for z in range(NZL)] for h in range(NZH)]
        order = [tiles[h][z][8 * c:8 * c + 8] for c in range(NK) for z in range(NZL) for h in range(NZH)]
        xt[:, pl.ds(pl.multiple_of(yy * 128, 128), 128)] = jnp.concatenate(order, axis=0).T.astype(BF16)
        return carry

    lax.fori_loop(0, NY, turn, 0)

    hop_arrivals(4, 1)
    pending["ring"], pending["gk"] = gb.at[pl.ds(0, 7), 0], gb.at[:, 0]
    normed_grad_terms(-3)
    normed_grad_terms(3)
    normed_grad_terms(4)
    pending["p"] = pb.at[:, pl.ds(0, 3)]

    def weight_grad(xx):
        g = gb[:, :, :, xx].reshape(1024, 384)
        return jnp.dot(xt[...], g, preferred_element_type=F32)

    x1, x2, x3 = at_x(1), at_x(2), at_x(3)
    gwp[x2] = weight_grad(x2).astype(BF16)
    send("gw_a", gwp.at[x2, pl.ds(0, 128)], gw1.at[0], dev(xx=x1))
    send("gw_b", gwp.at[x2, pl.ds(128, 128)], gw1.at[1], dev(xx=x3))
    for step in (0, -1, 1, -2, 2):
        normed_grad_sum(step)
    gwp[x1] = weight_grad(x1).astype(BF16)
    send("gw_c", gwp.at[x1, pl.ds(128, 128)], gw2.at[0, 1], dev(xx=x1))
    gwp[x3] = weight_grad(x3).astype(BF16)
    send("gw_d", gwp.at[x3, pl.ds(0, 128)], gw2.at[1, 0], dev(xx=x3))
    normed_grad_sum(-3)
    normed_grad_sum(3)
    normed_grad_sum(4)
    pending["f"] = xb.at[pl.ds(0, 15)]
    gw_own[...] = weight_grad(x)
    arrived("gw_a", gw1.at[0])
    gws[0] = (gwp[x1, 0:128].astype(F32) + gw1[0].astype(F32)).astype(BF16)
    send("gw_e", gws.at[0], gw2.at[0, 0], dev(xx=x1))
    arrived("gw_b", gw1.at[1])
    gws[1] = (gwp[x3, 128:256].astype(F32) + gw1[1].astype(F32)).astype(BF16)
    send("gw_f", gws.at[1], gw2.at[1, 1], dev(xx=x3))
    drain()
    arrived("gw_c", gw2.at[0, 1])
    arrived("gw_d", gw2.at[1, 0])
    arrived("gw_e", gw2.at[0, 0])
    arrived("gw_f", gw2.at[1, 1])
    for half in (0, 1):
        at = slice(128 * half, 128 * half + 128)
        total = gw_own[at] + gw2[0, half].astype(F32) + gw2[1, half].astype(F32)
        gkv_ref[at] = total[:, :128]
        gq_ref[at] = total[:, 128:]

    for s, o in far:
        arrived(("f", s, o), fr.at[at_y(-s), zls[o]])
    for b in range(NY * NZL):
        tile = fr[b // NZL, b % NZL].astype(F32)
        fk_keep[b] = jnp.where(k == 0, tile[:8], tile[8:])
        fk_send[b] = jnp.where(k == 0, tile[8:], tile[:8])
    send("fk", fk_send, fk_recv, core_peer)
    arrived("fk", fk_recv)
    dot = jnp.zeros((8, 256), F32)
    blocks = []
    for b in range(NY * NZL):
        keep, recv = fk_keep[b], fk_recv[b]
        for j, part in enumerate([jnp.where(k == 0, keep, recv), jnp.where(k == 0, recv, keep)]):
            cols = slice((2 * b + j) * 256, (2 * b + j + 1) * 256)
            scaled = part * gain_ref[:, cols]
            dot += scaled * unit_ref[:, cols]
            blocks.append((scaled, cols))
    mean = jnp.sum(dot, axis=-1, keepdims=True) * (1.0 / (256 * len(blocks)))
    for scaled, cols in blocks:
        dx_ref[:, cols] = (inv * (scaled - unit_ref[:, cols] * mean)).astype(BF16)
    drain()
    assert (len(send_names), len(recv_names)) == (N_SEND, N_RECV), (len(send_names), len(recv_names))


def on_device(block_input, norm_scale_weight, kv_weight, q_weight, kv_cotangent, q_cotangent):
    vmem = pl.BlockSpec(memory_space=pltpu.VMEM)
    hbm = pl.BlockSpec(memory_space=pltpu.HBM)

    def buf(dtype, *shape):
        return pltpu.VMEM(shape, dtype)

    return pl.pallas_call(
        kernel,
        out_shape=(
            jax.ShapeDtypeStruct((8, 8192), BF16),
            jax.ShapeDtypeStruct((256, 128), F32),
            jax.ShapeDtypeStruct((256, 256), F32),
        ),
        in_specs=[hbm] * 6,
        out_specs=(vmem,) * 3,
        scratch_shapes=[
            buf(BF16, 8, 8192), buf(F32, 1, 8192), buf(BF16, 256, 128), buf(BF16, 256, 256),
            buf(BF16, 128, 256), buf(BF16, 128, 256), buf(F32, 8, 8192),
            buf(F32, 16, 8, 256), buf(F32, 16, 8, 256), buf(F32, 16, 8, 256),
            buf(BF16, 16, 16, 256), buf(BF16, 4, 8, 2, 16, 256), buf(BF16, 256, 1024),
            buf(BF16, 4, 256, 384), buf(BF16, 4, 32, 128), buf(BF16, 4, 32, 128),
            buf(BF16, 4, 32, 384), buf(BF16, 8, 2, 2, 4, 32, 384),
            buf(BF16, 8, 4, 2, 16, 256), buf(BF16, 8, 4, 2, 16, 256),
            buf(BF16, 8, 2, 16, 256), buf(BF16, 8, 2, 16, 256),
            buf(F32, 16, 8, 256), buf(F32, 16, 8, 256), buf(F32, 16, 8, 256),
            buf(BF16, 4, 256, 384), buf(F32, 256, 384), buf(BF16, 2, 128, 384),
            buf(BF16, 2, 2, 128, 384), buf(BF16, 2, 128, 384),
            pltpu.SemaphoreType.DMA((6,)),
            pltpu.SemaphoreType.DMA((N_SEND,)), pltpu.SemaphoreType.DMA((N_RECV,)),
        ],
        compiler_params=pltpu.CompilerParams(
            collective_id=0, has_side_effects=True, vmem_limit_bytes=VL
        ),
        cost_estimate=pl.CostEstimate(flops=1_700_000_000, bytes_accessed=2_000_000, transcendentals=16),
        name="qkv_backward",
    )(
        block_input, norm_scale_weight.reshape(1, -1), kv_weight, q_weight,
        kv_cotangent.reshape(kv_cotangent.shape[0], -1), q_cotangent,
    )


def solution(mesh):
    in_specs = (
        P(("context", "tensor"), None),
        P(),
        P("context", "tensor"),
        P("context", "tensor"),
        P("context", "tensor", None),
        P("context", "tensor"),
    )
    out_specs = (P(("context", "tensor"), None), P("context", "tensor"), P("context", "tensor"))
    return jax.shard_map(
        on_device, mesh=mesh, in_specs=in_specs, out_specs=out_specs, check_vma=False
    )
```

time: 72.9 us -> 63 us (0.86)
  Pallas kernels: 64.8 us -> 59.2 us
  local copies, waits for them, and re-layouts: 7.09 us -> 2.98 us
    pallas_call x1, Pallas kernels: 64.8 us -> 59.2 us  [on_device(): pl.pallas_call(kernel, out_shape=(jax.ShapeDtypeStruct((8, 8192), BF16),...]
    unnamed x15 -> x7, local copies, waits for them, and re-layouts: 7.09 us -> 2.98 us
where the time goes in v3:
time: 63 us; the launch traced here: 62.8 us
  Pallas kernels  59.2 us (94%)
  local copies, waits for them, and re-layouts  2.98 us (5%)
  between operations  0.66 us (1%)
    pallas_call x1, Pallas kernels, on_device(): pl.pallas_call(kernel, out_shape=(jax.ShapeDtypeStruct((8, 8192), BF16),...  59.2 us
    unnamed x7, local copies, waits for them, and re-layouts  2.98 us

profile of v3, /device:TPU:1, one launch (start us, length us, event | category | flops | bytes accessed | tf_op | source)
XLA Modules:
  0.0 62.8 jit_solution(3682839628962705616)
XLA Ops:
  0.6 59.2 %qkv_backward.1 = (bf16[8,8192]{1,0:T(8,128)(2,1)}, f32[256,128]{1,0:T(8,128)}, f32[256,256]{1,0:T(8,128)}) custom-call(bf16[8,8192]{1,0:T(8,128)(2,1)} %x_hbm.1, f32[1,8192]{1,0:T(1,128)} %bitcast.3, bf16[256,128]{1,0:T(8,128)(2,1)} %kvw_hbm.1, bf16[256,256]{1,0:T(8,128)(2,1)} %qw_hbm.1, bf16[128,256]{1,0:T(8,128)(2,1)} %bitcast.2, bf16[128,256]{1,0:T(8,128)(2,1)} %qc_hbm.1), custom_call_target="tpu_custom_call" | custom-call | flops 1700000000 | bytes 2000000 | tf_op jit(solution)/shard_map/qkv_backward/pallas_call | solution.py:337
  59.8 0.0 copy-start.1
  59.8 0.0 copy-start
  59.8 1.6 %copy.12 = bf16[8,8192]{1,0:T(8,128)(2,1)} copy(bf16[8,8192]{1,0:T(8,128)(2,1)} %get-tuple-element.6) | data formatting | bytes 262144
  61.4 0.0 copy-done.1
  61.4 0.7 %copy.13 = f32[256,128]{1,0:T(8,128)} copy(f32[256,128]{1,0:T(8,128)S(1)} %copy-done.1) | data formatting | bytes 262144
  62.1 0.0 copy-done
  62.1 0.7 %copy.14 = f32[256,256]{1,0:T(8,128)} copy(f32[256,256]{1,0:T(8,128)S(1)} %copy-done) | data formatting | bytes 524288
Async XLA Ops:
  59.8 1.6 %copy-start.1 = (f32[256,128]{1,0:T(8,128)S(1)}, f32[256,128]{1,0:T(8,128)}, u32[]{:S(2)}) copy-start(f32[256,128]{1,0:T(8,128)} %get-tuple-element.7) | copy-start | bytes 393220
  59.8 2.3 %copy-start = (f32[256,256]{1,0:T(8,128)S(1)}, f32[256,256]{1,0:T(8,128)}, u32[]{:S(2)}) copy-start(f32[256,256]{1,0:T(8,128)} %get-tuple-element.8) | copy-start | bytes 786436

commit v4 on v3

v4 whole, which is shorter than its diff:
```python
import jax
import jax.numpy as jnp
from jax import lax
from jax.experimental import pallas as pl
from jax.experimental.pallas import tpu as pltpu
from jax.sharding import PartitionSpec as P

NY, NZL, NK = 8, 2, 2
NX, NZH = 4, 4
F32, BF16 = jnp.float32, jnp.bfloat16
N_SEND, N_RECV = 46, 196
VL = 63_400_000


def kernel(
    x_hbm, gain_hbm, kvw_hbm, qw_hbm, kvc_hbm, qc_hbm,
    dx_hbm, gkv_hbm, gq_hbm,
    dx_ref, gkv_ref, gq_ref,
    x_ref, gain_ref, kvw_ref, qw_ref, kvc_ref, qc_ref, unit_ref, scaled_ref,
    xk_keep, xk_send, xk_recv, xb, xg, xt,
    wb, va, ka, ks, kb, gq, gv,
    pb, pr, fb, fr, fk_keep, fk_send, fk_recv,
    gwp, gw_own, gw1, gw2, gws,
    load_sems, store_sems, send_sems, recv_sems,
):
    loads = [
        pltpu.make_async_copy(src, dst, load_sems.at[i])
        for i, (src, dst) in enumerate([
            (x_hbm, x_ref), (gain_hbm, gain_ref), (qc_hbm, qc_ref),
            (kvc_hbm, kvc_ref), (kvw_hbm, kvw_ref), (qw_hbm, qw_ref),
        ])
    ]
    for load in loads:
        load.start()

    context = lax.axis_index("context")
    tensor = lax.axis_index("tensor")
    y, zl, k = lax.div(context, NZL * NK), lax.rem(lax.div(context, NK), NZL), lax.rem(context, NK)
    x, zh = lax.div(tensor, NZH), lax.rem(tensor, NZH)
    ozl, ok = 1 - zl, 1 - k
    parity = lax.rem(zh, 2)
    ozh = zh + 1 - 2 * parity

    def at_y(step):
        return lax.rem(y + (step + NY) % NY, NY)

    def at_x(step):
        return lax.rem(x + (step + NX) % NX, NX)

    def at_zh(step):
        return lax.rem(zh + (step + NZH) % NZH, NZH)

    def dev(yy=y, zz=zl, kk=k, xx=x, hh=zh):
        return {"context": (yy * NZL + zz) * NK + kk, "tensor": xx * NZH + hh}

    zls = (zl, ozl)
    far = [(s, o) for s in range(NY) for o in range(2) if (s, o) != (0, 0)]
    core_peer = dev(kk=ok)
    right, left = dev(yy=at_y(1)), dev(yy=at_y(-1))

    recv_names, send_names = {}, {}

    steps = (0, 1, 7, 2, 6, 3, 5, 4)
    parts = ((0, 3), (3, 5), (5, 8))

    def send(name, src, dst, to, group=None):
        slot = recv_names.setdefault(name, len(recv_names))
        group = name if group is None else group
        sent = send_names.setdefault(group, len(send_names))
        pltpu.make_async_remote_copy(
            src_ref=src, dst_ref=dst, send_sem=send_sems.at[sent], recv_sem=recv_sems.at[slot],
            device_id=to, device_id_type=pl.DeviceIdType.MESH,
        ).start()
        pending.setdefault(group, src)

    def arrived(name, dst):
        slot = recv_names.setdefault(name, len(recv_names))
        pltpu.make_async_copy(dst, dst, recv_sems.at[slot]).wait()

    pending = {}

    def drain():
        for group, src in pending.items():
            pltpu.make_async_copy(src, src, send_sems.at[send_names[group]]).wait()
        pending.clear()

    peers = [dev(yy=at_y(s), zz=zls[o]) for s, o in far]
    peers += [dev(hh=at_zh(s)) for s in range(1, NZH)]
    peers += [dev(xx=at_x(s)) for s in range(1, NX)]
    peers += [dev(xx=at_x(s), hh=ozh) for s in range(1, NX)]
    peers += [core_peer]
    barrier = pltpu.get_barrier_semaphore()
    for peer in peers:
        pl.semaphore_signal(barrier, inc=1, device_id=peer, device_id_type=pl.DeviceIdType.MESH)

    def goes(hop, o, right_way, piece):
        return hop < 4 or (hop == 4 and right_way == ((piece in (0, 1, 2)) == (o == 0)))

    def ring_send(kind, buf, hop, o, at, piece):
        for right_way in (True, False):
            if goes(hop, o, right_way, piece):
                ref = buf.at[at_y(1 - hop if right_way else hop - 1), k, zls[o]].at[at]
                name = (kind + ("r" if right_way else "l"), hop, o, piece)
                send(name, ref, ref, right if right_way else left, kind + "ring" + str(o))

    def ring_q(hop, o, s):
        ring_send("q", gq, hop, o, s, s)

    def ring_v(hop, o):
        ring_send("v", gv, hop, o, pl.ds(0, NX), "v")

    def cross(kind, buf, at, piece):
        ref = buf.at[y, k, zl].at[at]
        send((kind + "z", piece), ref, ref, dev(zz=ozl), kind + "z")

    def start_q(s):
        ring_q(1, 0, s)
        cross("q", gq, s, s)

    def to_core(kind, buf, step, o):
        ref = buf.at[at_y(step), k, zls[o]]
        send((kind + "k", step, o), ref, ref, core_peer, kind + "k")

    loads[2].wait()
    loads[3].wait()
    gq[y, k, zl, 0] = qc_ref[pl.ds(pl.multiple_of(32 * x, 32), 32), :]
    for j in range(NX):
        part = kvc_ref[32 * j:32 * j + 32, :]
        keys, values = part[:, :128], part[:, 128:]
        va[j] = jnp.where(parity == 0, keys, values)
        ks[j] = jnp.where(parity == 0, values, keys)
    pl.semaphore_wait(barrier, len(peers))
    start_q(0)
    for s in (2, 1, 3):
        there = at_x(s)
        send(("qa", s), qc_ref.at[pl.ds(pl.multiple_of(32 * there, 32), 32)], gq.at[y, k, zl, s], dev(xx=there))
    for s in (2, 1, 3):
        send(("kb", s), ks.at[at_x(s)], kb.at[s], dev(xx=at_x(s), hh=ozh))
        send(("ka", s), va.at[at_x(s)], ka.at[s], dev(xx=at_x(s)))
    send(("kb", 0), ks.at[x], kb.at[0], dev(hh=ozh))
    ka[0] = va[x]

    loads[0].wait()
    loads[1].wait()
    rows = x_ref[...].astype(F32)
    inv = lax.rsqrt(jnp.mean(rows * rows, axis=-1, keepdims=True) + 1e-06)
    for b in range(NY * NZL):
        both = []
        for j in (0, 1):
            cols = slice((2 * b + j) * 256, (2 * b + j + 1) * 256)
            unit = rows[:, cols] * inv
            unit_ref[:, cols] = unit
            both.append((unit * gain_ref[:, cols]).astype(BF16).astype(F32))
        xk_keep[b] = jnp.where(k == 0, both[0], both[1])
        xk_send[b] = jnp.where(k == 0, both[1], both[0])
    send("xk", xk_send, xk_recv, core_peer)

    loads[4].wait()
    loads[5].wait()
    wb[0, :, :128] = kvw_ref[...]
    wb[0, :, 128:] = qw_ref[...]
    send("w_right", wb.at[0], wb.at[1], dev(xx=at_x(1)))
    send("w_left", wb.at[0], wb.at[3], dev(xx=at_x(-1)))

    arrived("xk", xk_recv)
    for b in range(NY * NZL):
        keep, recv = xk_keep[b], xk_recv[b]
        pair = [jnp.where(k == 0, keep, recv), jnp.where(k == 0, recv, keep)]
        xb[b] = jnp.concatenate(pair, axis=0).astype(BF16)
    for s, o in far:
        there = steps.index((-s) % NY)
        send(("xa", s, o), xb.at[at_y(s) * NZL + zls[o]], xg.at[zh, there, zl], dev(yy=at_y(s), zz=zls[o]), "xa")
    pending["xa"] = xb.at[pl.ds(0, 15)]
    xg[zh, 0, zl] = xb[y * NZL + zl]

    for s in (1, 3, 2):
        arrived(("qa", s), gq.at[y, k, zl, s])
        start_q(s)
    to_core("q", gq, 0, 0)

    def pass_on(kind, buf, hop, o, at, piece):
        steps = [step for step in ((-hop, hop) if hop < 4 else (4,))]
        for step in steps:
            right_way = goes(hop, o, True, piece) if hop == 4 else step < 0
            arrived((kind + ("r" if right_way else "l"), hop, o, piece), buf.at[at_y(step), k, zls[o]].at[at])
        ring_send(kind, buf, hop + 1, o, at, piece)

    def rows_part(p):
        first, last = parts[p]
        for n in range(first, last):
            for o in (0, 1):
                if (n, o) != (0, 0):
                    arrived(("xa", (-steps[n]) % NY, o), xg.at[zh, n, zls[o]])
        at = xg.at[zh, pl.ds(first, last - first)]
        send(("x_right", p), at, at, dev(hh=at_zh(1)))
        send(("x_left", p), at, at, dev(hh=at_zh(-1)))

    def rows_far(p):
        first, last = parts[p]
        for name, step, z, to in (("x_right", -1, 0, 1), ("x_left", 1, 1, -1)):
            arrived((name, p), xg.at[at_zh(step), pl.ds(first, last - first)])
            at = xg.at[at_zh(step), pl.ds(first, last - first), z]
            send((name, p, "far"), at, at, dev(hh=at_zh(to)))

    def hop_core(kind, buf, hop, o):
        if 0 < hop < 4:
            to_core(kind, buf, -hop, o)
        to_core(kind, buf, hop, o)

    def hop_q(hop, o):
        for s in (0, 1, 3, 2):
            pass_on("q", gq, hop, o, s, s)
        hop_core("q", gq, hop, o)

    def hop_v(hop, o):
        pass_on("v", gv, hop, o, pl.ds(0, NX), "v")
        hop_core("v", gv, hop, o)

    def crossed_q():
        for s in (0, 1, 3, 2):
            arrived(("qz", s), gq.at[y, k, ozl, s])
            ring_q(1, 1, s)
        to_core("q", gq, 0, 1)

    def crossed_v():
        arrived(("vz", "v"), gv.at[y, k, ozl])
        ring_v(1, 1)
        to_core("v", gv, 0, 1)

    def pair_heads():
        for s in range(NX):
            if s:
                arrived(("ka", s), ka.at[s])
            arrived(("kb", s), kb.at[s])
        gv[y, k, zl] = (ka[...].astype(F32) + kb[...].astype(F32)).astype(BF16)
        ring_v(1, 0)
        cross("v", gv, pl.ds(0, NX), "v")
        to_core("v", gv, 0, 0)

    def normed_grad_terms(step):
        yy = at_y(step)
        for o in (0, 1):
            arrived(("qk", step, o), gq.at[yy, ok, zls[o]])
            arrived(("vk", step, o), gv.at[yy, ok, zls[o]])
        acc = jnp.zeros((128, 256), F32)
        for j in range(NX):
            acc += lax.dot_general(
                gq[yy, :, :, j].reshape(128, 256), wb[j, :, 128:], (((1,), (1,)), ((), ())), preferred_element_type=F32
            )
            acc += lax.dot_general(
                gv[yy, :, :, j].reshape(128, 128), wb[j, :, :128], (((1,), (1,)), ((), ())), preferred_element_type=F32
            )
        for h in range(NZH):
            for z in range(NZL):
                start = z * 32 + h * 8
                pb[yy, h, z] = jnp.concatenate([acc[start:start + 8], acc[64 + start:72 + start]], axis=0).astype(BF16)
        for s in (2, 1, 3):
            send(("p", step, s), pb.at[yy, at_zh(s)], pr.at[yy, zh], dev(hh=at_zh(s)), "p")

    def normed_grad_sum(step):
        yy = at_y(step)
        for s in (1, 3, 2):
            arrived(("p", step, s), pr.at[yy, at_zh(-s)])
        total = pb[yy, zh].astype(F32)
        for s in (1, 2, 3):
            total += pr[yy, at_zh(s)].astype(F32)
        fb[yy] = total.astype(BF16)
        for o in (0, 1):
            if (step, o) != (0, 0):
                send(("f", step % NY, o), fb.at[yy, zls[o]], fr.at[y, zl], dev(yy=yy, zz=zls[o]), "f")
        if step == 0:
            fr[y, zl] = fb[y, zl]

    pair_heads()
    rows_part(0)
    hop_q(1, 0)
    crossed_q()

    arrived("w_right", wb.at[1])
    send("w_far0", wb.at[1, pl.ds(0, 128)], wb.at[2, pl.ds(0, 128)], dev(xx=at_x(1)))
    arrived("w_left", wb.at[3])
    send("w_far1", wb.at[3, pl.ds(128, 128)], wb.at[2, pl.ds(128, 128)], dev(xx=at_x(-1)))

    rows_part(1)
    hop_v(1, 0)
    crossed_v()
    rows_part(2)
    rows_far(0)
    hop_q(2, 0)
    hop_q(1, 1)
    hop_v(2, 0)
    hop_v(1, 1)
    rows_far(1)

    arrived("w_far0", wb.at[2, pl.ds(0, 128)])
    arrived("w_far1", wb.at[2, pl.ds(128, 128)])
    normed_grad_terms(0)
    hop_q(3, 0)
    rows_far(2)
    normed_grad_terms(-1)
    hop_q(2, 1)
    normed_grad_terms(1)
    hop_v(3, 0)
    hop_v(2, 1)
    hop_q(4, 0)
    hop_q(3, 1)
    hop_v(4, 0)
    normed_grad_terms(-2)
    hop_v(3, 1)
    normed_grad_terms(2)
    hop_q(4, 1)

    normed_grad_terms(-3)
    normed_grad_terms(3)
    hop_v(4, 1)
    pending["qk"], pending["vk"] = gq.at[:, 0], gv.at[:, 0]
    pending["qz"], pending["vz"] = gq.at[0, 0, 0], gv.at[0, 0, 0]
    pending["qring0"], pending["vring0"] = gq.at[pl.ds(0, 7), 0, 0], gv.at[pl.ds(0, 7), 0, 0]
    pending["qring1"], pending["vring1"] = gq.at[pl.ds(0, 7), 0, 0], gv.at[pl.ds(0, 7), 0, 0]
    normed_grad_terms(4)
    pending["p"] = pb.at[:, pl.ds(0, 3)]

    for p, (first, last) in enumerate(parts):
        for name, z in (("x_right", 0), ("x_left", 1)):
            arrived((name, p, "far"), xg.at[at_zh(2), pl.ds(first, last - first), z])

    def turn(n, yy):
        tiles = [[xg[h, n, z].astype(F32) for z in range(NZL)] for h in range(NZH)]
        order = [tiles[h][z][8 * c:8 * c + 8] for c in range(NK) for z in range(NZL) for h in range(NZH)]
        xt[:, pl.ds(pl.multiple_of(yy * 128, 128), 128)] = jnp.concatenate(order, axis=0).T.astype(BF16)

    for n, step in enumerate(steps):
        turn(n, at_y(step))

    def weight_grad(slot, out):
        value = jnp.dot(xt[...], gv[:, :, :, slot].reshape(1024, 128), preferred_element_type=F32)
        out[:, :128] = value.astype(out.dtype)
        query = jnp.dot(xt[...], gq[:, :, :, slot].reshape(1024, 256), preferred_element_type=F32)
        out[:, 128:] = query.astype(out.dtype)

    x1, x3 = at_x(1), at_x(-1)
    weight_grad(2, gwp.at[2])
    send("gw_a", gwp.at[2, pl.ds(0, 128)], gw1.at[0], dev(xx=x1))
    send("gw_b", gwp.at[2, pl.ds(128, 128)], gw1.at[1], dev(xx=x3))
    weight_grad(3, gwp.at[3])
    send("gw_c", gwp.at[3, pl.ds(128, 128)], gw2.at[0, 1], dev(xx=x1))
    weight_grad(1, gwp.at[1])
    send("gw_d", gwp.at[1, pl.ds(0, 128)], gw2.at[1, 0], dev(xx=x3))
    for step in (0, -1, 1, -2, 2):
        normed_grad_sum(step)
    normed_grad_sum(-3)
    normed_grad_sum(3)
    normed_grad_sum(4)
    pending["f"] = xb.at[pl.ds(0, 15)]
    arrived("gw_a", gw1.at[0])
    gws[0] = (gwp[3, 0:128].astype(F32) + gw1[0].astype(F32)).astype(BF16)
    send("gw_e", gws.at[0], gw2.at[0, 0], dev(xx=x1))
    arrived("gw_b", gw1.at[1])
    gws[1] = (gwp[1, 128:256].astype(F32) + gw1[1].astype(F32)).astype(BF16)
    send("gw_f", gws.at[1], gw2.at[1, 1], dev(xx=x3))
    weight_grad(0, gw_own)

    order = [(s, o) for s in steps for o in (0, 1)]
    groups = ((0, 10), (10, 16))

    def swap_cores(g):
        first, last = groups[g]
        for n in range(first, last):
            s, o = order[n]
            at = fr.at[at_y(-s), zls[o]]
            if (s, o) != (0, 0):
                arrived(("f", s, o), at)
            tile = at[...].astype(F32)
            fk_keep[n] = jnp.where(k == 0, tile[:8], tile[8:])
            fk_send[n] = jnp.where(k == 0, tile[8:], tile[:8])
        part = pl.ds(first, last - first)
        send(("fk", g), fk_send.at[part], fk_recv.at[part], core_peer)

    late = {name: pending.pop(name) for name in ("gw_e", "gw_f")}
    drain()
    pending.update(late)
    swap_cores(0)
    arrived("gw_c", gw2.at[0, 1])
    arrived("gw_d", gw2.at[1, 0])
    arrived("gw_e", gw2.at[0, 0])
    arrived("gw_f", gw2.at[1, 1])
    for half in (0, 1):
        at = slice(128 * half, 128 * half + 128)
        total = gw_own[at] + gw2[0, half].astype(F32) + gw2[1, half].astype(F32)
        gkv_ref[at] = total[:, :128]
        gq_ref[at] = total[:, 128:]
    stores = [
        pltpu.make_async_copy(src, dst, store_sems.at[i])
        for i, (src, dst) in enumerate([(gkv_ref, gkv_hbm), (gq_ref, gq_hbm), (dx_ref, dx_hbm)])
    ]
    stores[0].start()
    stores[1].start()

    swap_cores(1)
    dot = jnp.zeros((8, 512), F32)
    for g, (first, last) in enumerate(groups):
        arrived(("fk", g), fk_recv.at[pl.ds(first, last - first)])
        for n in range(first, last):
            s, o = order[n]
            cols = pl.ds(pl.multiple_of((at_y(-s) * NZL + zls[o]) * 512, 512), 512)
            keep, recv = fk_keep[n], fk_recv[n]
            pair = [jnp.where(k == 0, keep, recv), jnp.where(k == 0, recv, keep)]
            scaled = jnp.concatenate(pair, axis=1) * gain_ref[:, cols]
            scaled_ref[:, cols] = scaled
            dot += scaled * unit_ref[:, cols]
    mean = jnp.sum(dot, axis=-1, keepdims=True) * (1.0 / 8192)
    dx_ref[...] = (inv * (scaled_ref[...] - unit_ref[...] * mean)).astype(BF16)
    stores[2].start()
    drain()
    for store in stores:
        store.wait()
    assert (len(send_names), len(recv_names)) == (N_SEND, N_RECV), (len(send_names), len(recv_names))


def hand_over(*refs):
    for i in range(3):
        refs[3 + i][...] = refs[i][...]


def on_device(block_input, norm_scale_weight, kv_weight, q_weight, kv_cotangent, q_cotangent):
    hbm = pl.BlockSpec(memory_space=pltpu.HBM)
    vmem = pl.BlockSpec(memory_space=pltpu.VMEM)

    def buf(dtype, *shape):
        return pltpu.VMEM(shape, dtype)

    outs = pl.pallas_call(
        kernel,
        out_shape=(
            jax.ShapeDtypeStruct((8, 8192), BF16),
            jax.ShapeDtypeStruct((256, 128), F32),
            jax.ShapeDtypeStruct((256, 256), F32),
        ),
        in_specs=[hbm] * 6,
        out_specs=(hbm,) * 3,
        scratch_shapes=[
            buf(BF16, 8, 8192), buf(F32, 256, 128), buf(F32, 256, 256),
            buf(BF16, 8, 8192), buf(F32, 1, 8192), buf(BF16, 256, 128), buf(BF16, 256, 256),
            buf(BF16, 128, 256), buf(BF16, 128, 256), buf(F32, 8, 8192), buf(F32, 8, 8192),
            buf(F32, 16, 8, 256), buf(F32, 16, 8, 256), buf(F32, 16, 8, 256),
            buf(BF16, 16, 16, 256), buf(BF16, 4, 8, 2, 16, 256), buf(BF16, 256, 1024),
            buf(BF16, 4, 256, 384), buf(BF16, 4, 32, 128), buf(BF16, 4, 32, 128),
            buf(BF16, 4, 32, 128), buf(BF16, 4, 32, 128),
            buf(BF16, 8, 2, 2, 4, 32, 256), buf(BF16, 8, 2, 2, 4, 32, 128),
            buf(BF16, 8, 4, 2, 16, 256), buf(BF16, 8, 4, 2, 16, 256),
            buf(BF16, 8, 2, 16, 256), buf(BF16, 8, 2, 16, 256),
            buf(F32, 16, 8, 256), buf(F32, 16, 8, 256), buf(F32, 16, 8, 256),
            buf(BF16, 4, 256, 384), buf(F32, 256, 384), buf(BF16, 2, 128, 384),
            buf(BF16, 2, 2, 128, 384), buf(BF16, 2, 128, 384),
            pltpu.SemaphoreType.DMA((6,)), pltpu.SemaphoreType.DMA((3,)),
            pltpu.SemaphoreType.DMA((N_SEND,)), pltpu.SemaphoreType.DMA((N_RECV,)),
        ],
        compiler_params=pltpu.CompilerParams(
            collective_id=0, has_side_effects=True, vmem_limit_bytes=VL
        ),
        cost_estimate=pl.CostEstimate(flops=1_700_000_000, bytes_accessed=2_000_000, transcendentals=16),
        name="qkv_backward",
    )(
        block_input, norm_scale_weight.reshape(1, -1), kv_weight, q_weight,
        kv_cotangent.reshape(kv_cotangent.shape[0], -1), q_cotangent,
    )
    return pl.pallas_call(
        hand_over,
        out_shape=tuple(jax.ShapeDtypeStruct(out.shape, out.dtype) for out in outs),
        in_specs=[vmem] * 3,
        out_specs=(vmem,) * 3,
        compiler_params=pltpu.CompilerParams(vmem_limit_bytes=VL),
        name="hand_over",
    )(*outs)


def solution(mesh):
    in_specs = (
        P(("context", "tensor"), None),
        P(),
        P("context", "tensor"),
        P("context", "tensor"),
        P("context", "tensor", None),
        P("context", "tensor"),
    )
    out_specs = (P(("context", "tensor"), None), P("context", "tensor"), P("context", "tensor"))
    return jax.shard_map(
        on_device, mesh=mesh, in_specs=in_specs, out_specs=out_specs, check_vma=False
    )
```

time: 63 us -> 60.3 us (0.957)
  local copies, waits for them, and re-layouts: 2.98 us -> 0 us
    unnamed x7 -> x0, local copies, waits for them, and re-layouts: 2.98 us -> none
    pallas_call x0 -> x1, Pallas kernels: none -> 1.88 us  [on_device(): pl.pallas_call(hand_over, out_shape=tuple((jax.ShapeDtypeStruct(out.shape...]
    pallas_call x1, Pallas kernels: 59.2 us -> 57.6 us  [on_device(): pl.pallas_call(kernel, out_shape=(jax.ShapeDtypeStruct((8, 8192), BF16),...]
where the time goes in v4:
time: 60.3 us; the launch traced here: 60.2 us
  Pallas kernels  59.5 us (99%)
  between operations  0.64 us (1%)
    pallas_call x1, Pallas kernels, on_device(): pl.pallas_call(kernel, out_shape=(jax.ShapeDtypeStruct((8, 8192), BF16),...  57.6 us
    pallas_call x1, Pallas kernels, on_device(): pl.pallas_call(hand_over, out_shape=tuple((jax.ShapeDtypeStruct(out.shape...  1.88 us

profile of v4, /device:TPU:1, one launch (start us, length us, event | category | flops | bytes accessed | tf_op | source)
XLA Modules:
  0.0 60.2 jit_solution(7607213533876787959)
XLA Ops:
  0.6 57.6 %qkv_backward.1 = (bf16[8,8192]{1,0:T(8,128)(2,1)}, f32[256,128]{1,0:T(8,128)}, f32[256,256]{1,0:T(8,128)}) custom-call(bf16[8,8192]{1,0:T(8,128)(2,1)} %x_hbm.1, f32[1,8192]{1,0:T(1,128)} %bitcast.3, bf16[256,128]{1,0:T(8,128)(2,1)} %kvw_hbm.1, bf16[256,256]{1,0:T(8,128)(2,1)} %qw_hbm.1, bf16[128,256]{1,0:T(8,128)(2,1)} %bitcast.2, bf16[128,256]{1,0:T(8,128)(2,1)} %qc_hbm.1), custom_call_target="tpu_custom_call" | custom-call | flops 1700000000 | bytes 2000000 | tf_op jit(solution)/shard_map/qkv_backward/pallas_call | solution.py:432
  58.3 1.9 %hand_over.1 = (bf16[8,8192]{1,0:T(8,128)(2,1)}, f32[256,128]{1,0:T(8,128)}, f32[256,256]{1,0:T(8,128)}) custom-call(bf16[8,8192]{1,0:T(8,128)(2,1)} %get-tuple-element.6.refs_0_, f32[256,128]{1,0:T(8,128)} %get-tuple-element.7.refs_1_, f32[256,256]{1,0:T(8,128)} %get-tuple-element.8.refs_2_), custom_call_target="tpu_custom_call" | custom-call | tf_op jit(solution)/shard_map/hand_over/pallas_call | solution.py:467

commit v5 on v4

--- a/solution.py
+++ b/solution.py
@@ -8,19 +8,18 @@
 NY, NZL, NK = 8, 2, 2
 NX, NZH = 4, 4
 F32, BF16 = jnp.float32, jnp.bfloat16
-N_SEND, N_RECV = 46, 196
+N_SEND, N_RECV = 17, 136
 VL = 63_400_000
 
 
 def kernel(
     x_hbm, gain_hbm, kvw_hbm, qw_hbm, kvc_hbm, qc_hbm,
-    dx_hbm, gkv_hbm, gq_hbm,
-    dx_ref, gkv_ref, gq_ref,
-    x_ref, gain_ref, kvw_ref, qw_ref, kvc_ref, qc_ref, unit_ref, scaled_ref,
+    dn_hbm, own_hbm, gw2,
+    x_ref, gain_ref, kvw_ref, qw_ref, kvc_ref, qc_ref,
     xk_keep, xk_send, xk_recv, xb, xg, xt,
     wb, va, ka, ks, kb, gq, gv,
-    pb, pr, fb, fr, fk_keep, fk_send, fk_recv,
-    gwp, gw_own, gw1, gw2, gws,
+    pb, pr, fb, fr, fk_keep, fk_send,
+    gwp, gw_own, gw1, gws,
     load_sems, store_sems, send_sems, recv_sems,
 ):
     loads = [
@@ -101,7 +100,7 @@
             if goes(hop, o, right_way, piece):
                 ref = buf.at[at_y(1 - hop if right_way else hop - 1), k, zls[o]].at[at]
                 name = (kind + ("r" if right_way else "l"), hop, o, piece)
-                send(name, ref, ref, right if right_way else left, kind + "ring" + str(o))
+                send(name, ref, ref, right if right_way else left, kind + "ring")
 
     def ring_q(hop, o, s):
         ring_send("q", gq, hop, o, s, s)
@@ -119,7 +118,7 @@
 
     def to_core(kind, buf, step, o):
         ref = buf.at[at_y(step), k, zls[o]]
-        send((kind + "k", step, o), ref, ref, core_peer, kind + "k")
+        send(("k", step), ref, ref, core_peer, kind + "k")
 
     loads[2].wait()
     loads[3].wait()
@@ -133,11 +132,11 @@
     start_q(0)
     for s in (2, 1, 3):
         there = at_x(s)
-        send(("qa", s), qc_ref.at[pl.ds(pl.multiple_of(32 * there, 32), 32)], gq.at[y, k, zl, s], dev(xx=there))
+        send(("qa", s), qc_ref.at[pl.ds(pl.multiple_of(32 * there, 32), 32)], gq.at[y, k, zl, s], dev(xx=there), "qa")
     for s in (2, 1, 3):
-        send(("kb", s), ks.at[at_x(s)], kb.at[s], dev(xx=at_x(s), hh=ozh))
-        send(("ka", s), va.at[at_x(s)], ka.at[s], dev(xx=at_x(s)))
-    send(("kb", 0), ks.at[x], kb.at[0], dev(hh=ozh))
+        send(("kb", s), ks.at[at_x(s)], kb.at[s], dev(xx=at_x(s), hh=ozh), "kb")
+        send(("ka", s), va.at[at_x(s)], ka.at[s], dev(xx=at_x(s)), "ka")
+    send(("kb", 0), ks.at[x], kb.at[0], dev(hh=ozh), "kb")
     ka[0] = va[x]
 
     loads[0].wait()
@@ -149,7 +148,6 @@
         for j in (0, 1):
             cols = slice((2 * b + j) * 256, (2 * b + j + 1) * 256)
             unit = rows[:, cols] * inv
-            unit_ref[:, cols] = unit
             both.append((unit * gain_ref[:, cols]).astype(BF16).astype(F32))
         xk_keep[b] = jnp.where(k == 0, both[0], both[1])
         xk_send[b] = jnp.where(k == 0, both[1], both[0])
@@ -159,8 +157,8 @@
     loads[5].wait()
     wb[0, :, :128] = kvw_ref[...]
     wb[0, :, 128:] = qw_ref[...]
-    send("w_right", wb.at[0], wb.at[1], dev(xx=at_x(1)))
-    send("w_left", wb.at[0], wb.at[3], dev(xx=at_x(-1)))
+    send("w_right", wb.at[0], wb.at[1], dev(xx=at_x(1)), "w")
+    send("w_left", wb.at[0], wb.at[3], dev(xx=at_x(-1)), "w")
 
     arrived("xk", xk_recv)
     for b in range(NY * NZL):
@@ -169,7 +167,7 @@
         xb[b] = jnp.concatenate(pair, axis=0).astype(BF16)
     for s, o in far:
         there = steps.index((-s) % NY)
-        send(("xa", s, o), xb.at[at_y(s) * NZL + zls[o]], xg.at[zh, there, zl], dev(yy=at_y(s), zz=zls[o]), "xa")
+        send(("xa", [first <= there < last for first, last in parts].index(True)), xb.at[at_y(s) * NZL + zls[o]], xg.at[zh, there, zl], dev(yy=at_y(s), zz=zls[o]), "xa")
     pending["xa"] = xb.at[pl.ds(0, 15)]
     xg[zh, 0, zl] = xb[y * NZL + zl]
 
@@ -187,20 +185,17 @@
 
     def rows_part(p):
         first, last = parts[p]
-        for n in range(first, last):
-            for o in (0, 1):
-                if (n, o) != (0, 0):
-                    arrived(("xa", (-steps[n]) % NY, o), xg.at[zh, n, zls[o]])
+        arrived(("xa", p), xb.at[pl.ds(0, 2 * (last - first) - (p == 0))])
         at = xg.at[zh, pl.ds(first, last - first)]
-        send(("x_right", p), at, at, dev(hh=at_zh(1)))
-        send(("x_left", p), at, at, dev(hh=at_zh(-1)))
+        send(("x_right", p), at, at, dev(hh=at_zh(1)), "x")
+        send(("x_left", p), at, at, dev(hh=at_zh(-1)), "x")
 
     def rows_far(p):
         first, last = parts[p]
         for name, step, z, to in (("x_right", -1, 0, 1), ("x_left", 1, 1, -1)):
             arrived((name, p), xg.at[at_zh(step), pl.ds(first, last - first)])
             at = xg.at[at_zh(step), pl.ds(first, last - first), z]
-            send((name, p, "far"), at, at, dev(hh=at_zh(to)))
+            send((name, p, "far"), at, at, dev(hh=at_zh(to)), "x")
 
     def hop_core(kind, buf, hop, o):
         if 0 < hop < 4:
@@ -239,9 +234,7 @@
 
     def normed_grad_terms(step):
         yy = at_y(step)
-        for o in (0, 1):
-            arrived(("qk", step, o), gq.at[yy, ok, zls[o]])
-            arrived(("vk", step, o), gv.at[yy, ok, zls[o]])
+        arrived(("k", step), gq.at[pl.ds(0, 3), 0, 0])
         acc = jnp.zeros((128, 256), F32)
         for j in range(NX):
             acc += lax.dot_general(
@@ -255,19 +248,18 @@
                 start = z * 32 + h * 8
                 pb[yy, h, z] = jnp.concatenate([acc[start:start + 8], acc[64 + start:72 + start]], axis=0).astype(BF16)
         for s in (2, 1, 3):
-            send(("p", step, s), pb.at[yy, at_zh(s)], pr.at[yy, zh], dev(hh=at_zh(s)), "p")
+            send(("p", step), pb.at[yy, at_zh(s)], pr.at[yy, zh], dev(hh=at_zh(s)), "p")
 
     def normed_grad_sum(step):
         yy = at_y(step)
-        for s in (1, 3, 2):
-            arrived(("p", step, s), pr.at[yy, at_zh(-s)])
+        arrived(("p", step), pr.at[yy, pl.ds(0, 3)])
         total = pb[yy, zh].astype(F32)
         for s in (1, 2, 3):
             total += pr[yy, at_zh(s)].astype(F32)
         fb[yy] = total.astype(BF16)
         for o in (0, 1):
             if (step, o) != (0, 0):
-                send(("f", step % NY, o), fb.at[yy, zls[o]], fr.at[y, zl], dev(yy=yy, zz=zls[o]), "f")
+                send(("f", step % NY), fb.at[yy, zls[o]], fr.at[y, zl], dev(yy=yy, zz=zls[o]), "f")
         if step == 0:
             fr[y, zl] = fb[y, zl]
 
@@ -277,31 +269,31 @@
     crossed_q()
 
     arrived("w_right", wb.at[1])
-    send("w_far0", wb.at[1, pl.ds(0, 128)], wb.at[2, pl.ds(0, 128)], dev(xx=at_x(1)))
+    send("w_far0", wb.at[1, pl.ds(0, 128)], wb.at[2, pl.ds(0, 128)], dev(xx=at_x(1)), "w")
     arrived("w_left", wb.at[3])
-    send("w_far1", wb.at[3, pl.ds(128, 128)], wb.at[2, pl.ds(128, 128)], dev(xx=at_x(-1)))
+    send("w_far1", wb.at[3, pl.ds(128, 128)], wb.at[2, pl.ds(128, 128)], dev(xx=at_x(-1)), "w")
 
     rows_part(1)
     hop_v(1, 0)
     crossed_v()
     rows_part(2)
-    rows_far(0)
     hop_q(2, 0)
     hop_q(1, 1)
+    rows_far(0)
     hop_v(2, 0)
     hop_v(1, 1)
-    rows_far(1)
 
     arrived("w_far0", wb.at[2, pl.ds(0, 128)])
     arrived("w_far1", wb.at[2, pl.ds(128, 128)])
     normed_grad_terms(0)
     hop_q(3, 0)
-    rows_far(2)
+    hop_q(2, 1)
+    rows_far(1)
     normed_grad_terms(-1)
-    hop_q(2, 1)
-    normed_grad_terms(1)
     hop_v(3, 0)
     hop_v(2, 1)
+    rows_far(2)
+    normed_grad_terms(1)
     hop_q(4, 0)
     hop_q(3, 1)
     hop_v(4, 0)
@@ -315,8 +307,9 @@
     hop_v(4, 1)
     pending["qk"], pending["vk"] = gq.at[:, 0], gv.at[:, 0]
     pending["qz"], pending["vz"] = gq.at[0, 0, 0], gv.at[0, 0, 0]
-    pending["qring0"], pending["vring0"] = gq.at[pl.ds(0, 7), 0, 0], gv.at[pl.ds(0, 7), 0, 0]
-    pending["qring1"], pending["vring1"] = gq.at[pl.ds(0, 7), 0, 0], gv.at[pl.ds(0, 7), 0, 0]
+    pending["qring"], pending["vring"] = gq.at[pl.ds(0, 7), 0], gv.at[pl.ds(0, 7), 0]
+    pending["w"], pending["x"] = wb.at[pl.ds(0, 3)], xg.at[pl.ds(0, 3)]
+    pending["qa"], pending["ka"], pending["kb"] = gq.at[0, 0, 0, pl.ds(0, 3)], va.at[pl.ds(0, 3)], ks
     normed_grad_terms(4)
     pending["p"] = pb.at[:, pl.ds(0, 3)]
 
@@ -340,12 +333,12 @@
 
     x1, x3 = at_x(1), at_x(-1)
     weight_grad(2, gwp.at[2])
-    send("gw_a", gwp.at[2, pl.ds(0, 128)], gw1.at[0], dev(xx=x1))
-    send("gw_b", gwp.at[2, pl.ds(128, 128)], gw1.at[1], dev(xx=x3))
+    send("gw_a", gwp.at[2, pl.ds(0, 128)], gw1.at[0], dev(xx=x1), "gw")
+    send("gw_b", gwp.at[2, pl.ds(128, 128)], gw1.at[1], dev(xx=x3), "gw")
     weight_grad(3, gwp.at[3])
-    send("gw_c", gwp.at[3, pl.ds(128, 128)], gw2.at[0, 1], dev(xx=x1))
+    send("gw_c", gwp.at[3, pl.ds(128, 128)], gw2.at[0, 1], dev(xx=x1), "gw")
     weight_grad(1, gwp.at[1])
-    send("gw_d", gwp.at[1, pl.ds(0, 128)], gw2.at[1, 0], dev(xx=x3))
+    send("gw_d", gwp.at[1, pl.ds(0, 128)], gw2.at[1, 0], dev(xx=x3), "gw")
     for step in (0, -1, 1, -2, 2):
         normed_grad_sum(step)
     normed_grad_sum(-3)
@@ -354,72 +347,64 @@
     pending["f"] = xb.at[pl.ds(0, 15)]
     arrived("gw_a", gw1.at[0])
     gws[0] = (gwp[3, 0:128].astype(F32) + gw1[0].astype(F32)).astype(BF16)
-    send("gw_e", gws.at[0], gw2.at[0, 0], dev(xx=x1))
+    send("gw_e", gws.at[0], gw2.at[0, 0], dev(xx=x1), "gw")
     arrived("gw_b", gw1.at[1])
     gws[1] = (gwp[1, 128:256].astype(F32) + gw1[1].astype(F32)).astype(BF16)
-    send("gw_f", gws.at[1], gw2.at[1, 1], dev(xx=x3))
+    send("gw_f", gws.at[1], gw2.at[1, 1], dev(xx=x3), "gw")
     weight_grad(0, gw_own)
-
-    order = [(s, o) for s in steps for o in (0, 1)]
-    groups = ((0, 10), (10, 16))
-
-    def swap_cores(g):
-        first, last = groups[g]
-        for n in range(first, last):
-            s, o = order[n]
-            at = fr.at[at_y(-s), zls[o]]
-            if (s, o) != (0, 0):
-                arrived(("f", s, o), at)
+    stores = [pltpu.make_async_copy(gw_own, own_hbm, store_sems.at[1])]
+    stores[0].start()
+
+    def swap_cores(n):
+        step = steps[n]
+        arrived(("f", step), fr.at[0] if step else fr.at[0, 0])
+        for o in (0, 1):
+            at = fr.at[at_y(-step), zls[o]]
             tile = at[...].astype(F32)
-            fk_keep[n] = jnp.where(k == 0, tile[:8], tile[8:])
-            fk_send[n] = jnp.where(k == 0, tile[8:], tile[:8])
-        part = pl.ds(first, last - first)
-        send(("fk", g), fk_send.at[part], fk_recv.at[part], core_peer)
-
-    late = {name: pending.pop(name) for name in ("gw_e", "gw_f")}
+            fk_keep[n, zls[o]] = jnp.where(k == 0, tile[:8], tile[8:])
+            fk_send[n, zls[o]] = jnp.where(k == 0, tile[8:], tile[:8])
+        there = dn_hbm.at[at_y(-step), :, k]
+        send("fk", fk_send.at[n], there, core_peer)
+        pltpu.make_async_copy(fk_keep.at[n], there, store_sems.at[0]).start()
+
+    del pending["gw"]
     drain()
-    pending.update(late)
-    swap_cores(0)
+    pending["gw"] = gwp.at[pl.ds(0, 3)]
+    for n in range(5):
+        swap_cores(n)
+    for n in range(5, 8):
+        swap_cores(n)
+    pending["fk"] = fk_send
+    drain()
+    stores[0].wait()
+    pltpu.make_async_copy(fk_keep, fk_keep, store_sems.at[0]).wait()
+    arrived("fk", fk_send)
     arrived("gw_c", gw2.at[0, 1])
     arrived("gw_d", gw2.at[1, 0])
     arrived("gw_e", gw2.at[0, 0])
     arrived("gw_f", gw2.at[1, 1])
+    assert (len(send_names), len(recv_names)) == (N_SEND, N_RECV), (len(send_names), len(recv_names))
+
+
+def finish(x_ref, gain_ref, dn_ref, own_ref, gw_ref, dx_ref, gkv_ref, gq_ref):
     for half in (0, 1):
         at = slice(128 * half, 128 * half + 128)
-        total = gw_own[at] + gw2[0, half].astype(F32) + gw2[1, half].astype(F32)
+        total = own_ref[at] + gw_ref[0, half].astype(F32) + gw_ref[1, half].astype(F32)
         gkv_ref[at] = total[:, :128]
         gq_ref[at] = total[:, 128:]
-    stores = [
-        pltpu.make_async_copy(src, dst, store_sems.at[i])
-        for i, (src, dst) in enumerate([(gkv_ref, gkv_hbm), (gq_ref, gq_hbm), (dx_ref, dx_hbm)])
-    ]
-    stores[0].start()
-    stores[1].start()
-
-    swap_cores(1)
-    dot = jnp.zeros((8, 512), F32)
-    for g, (first, last) in enumerate(groups):
-        arrived(("fk", g), fk_recv.at[pl.ds(first, last - first)])
-        for n in range(first, last):
-            s, o = order[n]
-            cols = pl.ds(pl.multiple_of((at_y(-s) * NZL + zls[o]) * 512, 512), 512)
-            keep, recv = fk_keep[n], fk_recv[n]
-            pair = [jnp.where(k == 0, keep, recv), jnp.where(k == 0, recv, keep)]
-            scaled = jnp.concatenate(pair, axis=1) * gain_ref[:, cols]
-            scaled_ref[:, cols] = scaled
-            dot += scaled * unit_ref[:, cols]
+    rows = x_ref[...].astype(F32)
+    inv = lax.rsqrt(jnp.mean(rows * rows, axis=-1, keepdims=True) + 1e-06)
+    dot = jnp.zeros((8, 256), F32)
+    blocks = []
+    for b in range(NY * NZL * NK):
+        cols = slice(256 * b, 256 * b + 256)
+        scaled = gain_ref[:, cols] * dn_ref[b // 4, b // 2 % 2, b % 2]
+        unit = rows[:, cols] * inv
+        dot += scaled * unit
+        blocks.append((cols, scaled, unit))
     mean = jnp.sum(dot, axis=-1, keepdims=True) * (1.0 / 8192)
-    dx_ref[...] = (inv * (scaled_ref[...] - unit_ref[...] * mean)).astype(BF16)
-    stores[2].start()
-    drain()
-    for store in stores:
-        store.wait()
-    assert (len(send_names), len(recv_names)) == (N_SEND, N_RECV), (len(send_names), len(recv_names))
-
-
-def hand_over(*refs):
-    for i in range(3):
-        refs[3 + i][...] = refs[i][...]
+    for cols, scaled, unit in blocks:
+        dx_ref[:, cols] = (inv * (scaled - unit * mean)).astype(BF16)
 
 
 def on_device(block_input, norm_scale_weight, kv_weight, q_weight, kv_cotangent, q_cotangent):
@@ -429,19 +414,19 @@
     def buf(dtype, *shape):
         return pltpu.VMEM(shape, dtype)
 
-    outs = pl.pallas_call(
+    gain = norm_scale_weight.reshape(1, -1)
+    dn, own, gw2 = pl.pallas_call(
         kernel,
         out_shape=(
-            jax.ShapeDtypeStruct((8, 8192), BF16),
-            jax.ShapeDtypeStruct((256, 128), F32),
-            jax.ShapeDtypeStruct((256, 256), F32),
+            jax.ShapeDtypeStruct((NY, NZL, NK, 8, 256), F32),
+            jax.ShapeDtypeStruct((256, 384), F32),
+            jax.ShapeDtypeStruct((2, 2, 128, 384), BF16),
         ),
         in_specs=[hbm] * 6,
         out_specs=(hbm,) * 3,
         scratch_shapes=[
-            buf(BF16, 8, 8192), buf(F32, 256, 128), buf(F32, 256, 256),
             buf(BF16, 8, 8192), buf(F32, 1, 8192), buf(BF16, 256, 128), buf(BF16, 256, 256),
-            buf(BF16, 128, 256), buf(BF16, 128, 256), buf(F32, 8, 8192), buf(F32, 8, 8192),
+            buf(BF16, 128, 256), buf(BF16, 128, 256),
             buf(F32, 16, 8, 256), buf(F32, 16, 8, 256), buf(F32, 16, 8, 256),
             buf(BF16, 16, 16, 256), buf(BF16, 4, 8, 2, 16, 256), buf(BF16, 256, 1024),
             buf(BF16, 4, 256, 384), buf(BF16, 4, 32, 128), buf(BF16, 4, 32, 128),
@@ -449,10 +434,10 @@
             buf(BF16, 8, 2, 2, 4, 32, 256), buf(BF16, 8, 2, 2, 4, 32, 128),
             buf(BF16, 8, 4, 2, 16, 256), buf(BF16, 8, 4, 2, 16, 256),
             buf(BF16, 8, 2, 16, 256), buf(BF16, 8, 2, 16, 256),
-            buf(F32, 16, 8, 256), buf(F32, 16, 8, 256), buf(F32, 16, 8, 256),
+            buf(F32, 8, 2, 8, 256), buf(F32, 8, 2, 8, 256),
             buf(BF16, 4, 256, 384), buf(F32, 256, 384), buf(BF16, 2, 128, 384),
-            buf(BF16, 2, 2, 128, 384), buf(BF16, 2, 128, 384),
-            pltpu.SemaphoreType.DMA((6,)), pltpu.SemaphoreType.DMA((3,)),
+            buf(BF16, 2, 128, 384),
+            pltpu.SemaphoreType.DMA((6,)), pltpu.SemaphoreType.DMA((2,)),
             pltpu.SemaphoreType.DMA((N_SEND,)), pltpu.SemaphoreType.DMA((N_RECV,)),
         ],
         compiler_params=pltpu.CompilerParams(
@@ -461,17 +446,21 @@
         cost_estimate=pl.CostEstimate(flops=1_700_000_000, bytes_accessed=2_000_000, transcendentals=16),
         name="qkv_backward",
     )(
-        block_input, norm_scale_weight.reshape(1, -1), kv_weight, q_weight,
+        block_input, gain, kv_weight, q_weight,
         kv_cotangent.reshape(kv_cotangent.shape[0], -1), q_cotangent,
     )
     return pl.pallas_call(
-        hand_over,
-        out_shape=tuple(jax.ShapeDtypeStruct(out.shape, out.dtype) for out in outs),
-        in_specs=[vmem] * 3,
+        finish,
+        out_shape=(
+            jax.ShapeDtypeStruct((8, 8192), BF16),
+            jax.ShapeDtypeStruct((256, 128), F32),
+            jax.ShapeDtypeStruct((256, 256), F32),
+        ),
+        in_specs=[vmem] * 5,
         out_specs=(vmem,) * 3,
         compiler_params=pltpu.CompilerParams(vmem_limit_bytes=VL),
-        name="hand_over",
-    )(*outs)
+        name="finish",
+    )(block_input, gain, dn, own, gw2)
 
 
 def solution(mesh):

time: 60.3 us -> 57.9 us (0.960)
  Pallas kernels: 59.5 us -> 57.1 us
    pallas_call x2, Pallas kernels: 59.5 us -> 57.1 us  [the longest x1 54.8 us: on_device(): pl.pallas_call(kernel, out_shape=(jax.ShapeDtypeStruct((NY, NZL, NK, 8, 2...]
where the time goes in v5:
time: 57.9 us; the launch traced here: 57.7 us
  Pallas kernels  57.1 us (99%)
  between operations  0.64 us (1%)
    pallas_call x1, Pallas kernels, on_device(): pl.pallas_call(kernel, out_shape=(jax.ShapeDtypeStruct((NY, NZL, NK, 8, 2...  54.8 us
    pallas_call x1, Pallas kernels, on_device(): pl.pallas_call(finish, out_shape=(jax.ShapeDtypeStruct((8, 8192), BF16),...  2.28 us

profile of v5, /device:TPU:1, one launch (start us, length us, event | category | flops | bytes accessed | tf_op | source)
XLA Modules:
  0.0 57.7 jit_solution(13315425835856719863)
XLA Ops:
  0.6 54.8 %qkv_backward.1 = (f32[8,2,2,8,256]{4,3,2,1,0:T(8,128)}, f32[256,384]{1,0:T(8,128)}, bf16[2,2,128,384]{3,2,1,0:T(8,128)(2,1)}) custom-call(bf16[8,8192]{1,0:T(8,128)(2,1)} %x_ref.1, f32[1,8192]{1,0:T(1,128)} %bitcast.2, bf16[256,128]{1,0:T(8,128)(2,1)} %kvw_hbm.1, bf16[256,256]{1,0:T(8,128)(2,1)} %qw_hbm.1, bf16[128,256]{1,0:T(8,128)(2,1)} %bitcast.4, ...), custom_call_target="tpu_custom_call" | custom-call | flops 1700000000 | bytes 2000000 | tf_op jit(solution)/shard_map/qkv_backward/pallas_call | solution.py:418
  55.4 2.3 %finish.1 = (bf16[8,8192]{1,0:T(8,128)(2,1)}, f32[256,128]{1,0:T(8,128)}, f32[256,256]{1,0:T(8,128)}) custom-call(bf16[8,8192]{1,0:T(8,128)(2,1)} %x_ref.1, f32[1,8192]{1,0:T(1,128)} %bitcast.3, f32[8,2,2,8,256]{4,3,2,1,0:T(8,128)} %get-tuple-element.6.dn_ref, f32[256,384]{1,0:T(8,128)} %get-tuple-element.7.own_ref, ...), custom_call_target="tpu_custom_call" | custom-call | tf_op jit(solution)/shard_map/finish/pallas_call | solution.py:452

commit v6 on v5

--- a/solution.py
+++ b/solution.py
@@ -8,7 +8,7 @@
 NY, NZL, NK = 8, 2, 2
 NX, NZH = 4, 4
 F32, BF16 = jnp.float32, jnp.bfloat16
-N_SEND, N_RECV = 17, 136
+N_SEND, N_RECV = 17, 120
 VL = 63_400_000
 
 
@@ -60,7 +60,7 @@
     recv_names, send_names = {}, {}
 
     steps = (0, 1, 7, 2, 6, 3, 5, 4)
-    parts = ((0, 3), (3, 5), (5, 8))
+    parts = ((0, 5), (5, 8))
 
     def send(name, src, dst, to, group=None):
         slot = recv_names.setdefault(name, len(recv_names))
@@ -134,9 +134,9 @@
         there = at_x(s)
         send(("qa", s), qc_ref.at[pl.ds(pl.multiple_of(32 * there, 32), 32)], gq.at[y, k, zl, s], dev(xx=there), "qa")
     for s in (2, 1, 3):
-        send(("kb", s), ks.at[at_x(s)], kb.at[s], dev(xx=at_x(s), hh=ozh), "kb")
-        send(("ka", s), va.at[at_x(s)], ka.at[s], dev(xx=at_x(s)), "ka")
-    send(("kb", 0), ks.at[x], kb.at[0], dev(hh=ozh), "kb")
+        send("kb", ks.at[at_x(s)], kb.at[s], dev(xx=at_x(s), hh=ozh), "kb")
+        send("ka", va.at[at_x(s)], ka.at[s], dev(xx=at_x(s)), "ka")
+    send("kb", ks.at[x], kb.at[0], dev(hh=ozh), "kb")
     ka[0] = va[x]
 
     loads[0].wait()
@@ -195,7 +195,7 @@
         for name, step, z, to in (("x_right", -1, 0, 1), ("x_left", 1, 1, -1)):
             arrived((name, p), xg.at[at_zh(step), pl.ds(first, last - first)])
             at = xg.at[at_zh(step), pl.ds(first, last - first), z]
-            send((name, p, "far"), at, at, dev(hh=at_zh(to)), "x")
+            send(("far", p), at, at, dev(hh=at_zh(to)), "x")
 
     def hop_core(kind, buf, hop, o):
         if 0 < hop < 4:
@@ -223,10 +223,8 @@
         to_core("v", gv, 0, 1)
 
     def pair_heads():
-        for s in range(NX):
-            if s:
-                arrived(("ka", s), ka.at[s])
-            arrived(("kb", s), kb.at[s])
+        arrived("ka", ka.at[pl.ds(1, 3)])
+        arrived("kb", kb)
         gv[y, k, zl] = (ka[...].astype(F32) + kb[...].astype(F32)).astype(BF16)
         ring_v(1, 0)
         cross("v", gv, pl.ds(0, NX), "v")
@@ -269,30 +267,27 @@
     crossed_q()
 
     arrived("w_right", wb.at[1])
-    send("w_far0", wb.at[1, pl.ds(0, 128)], wb.at[2, pl.ds(0, 128)], dev(xx=at_x(1)), "w")
+    send("w_far", wb.at[1, pl.ds(0, 128)], wb.at[2, pl.ds(0, 128)], dev(xx=at_x(1)), "w")
     arrived("w_left", wb.at[3])
-    send("w_far1", wb.at[3, pl.ds(128, 128)], wb.at[2, pl.ds(128, 128)], dev(xx=at_x(-1)), "w")
-
-    rows_part(1)
+    send("w_far", wb.at[3, pl.ds(128, 128)], wb.at[2, pl.ds(128, 128)], dev(xx=at_x(-1)), "w")
+
     hop_v(1, 0)
     crossed_v()
-    rows_part(2)
+    rows_part(1)
     hop_q(2, 0)
     hop_q(1, 1)
     rows_far(0)
     hop_v(2, 0)
     hop_v(1, 1)
 
-    arrived("w_far0", wb.at[2, pl.ds(0, 128)])
-    arrived("w_far1", wb.at[2, pl.ds(128, 128)])
+    arrived("w_far", wb.at[2])
     normed_grad_terms(0)
     hop_q(3, 0)
     hop_q(2, 1)
-    rows_far(1)
     normed_grad_terms(-1)
     hop_v(3, 0)
     hop_v(2, 1)
-    rows_far(2)
+    rows_far(1)
     normed_grad_terms(1)
     hop_q(4, 0)
     hop_q(3, 1)
@@ -314,8 +309,7 @@
     pending["p"] = pb.at[:, pl.ds(0, 3)]
 
     for p, (first, last) in enumerate(parts):
-        for name, z in (("x_right", 0), ("x_left", 1)):
-            arrived((name, p, "far"), xg.at[at_zh(2), pl.ds(first, last - first), z])
+        arrived(("far", p), xg.at[at_zh(2), pl.ds(first, last - first)])
 
     def turn(n, yy):
         tiles = [[xg[h, n, z].astype(F32) for z in range(NZL)] for h in range(NZH)]
@@ -336,9 +330,9 @@
     send("gw_a", gwp.at[2, pl.ds(0, 128)], gw1.at[0], dev(xx=x1), "gw")
     send("gw_b", gwp.at[2, pl.ds(128, 128)], gw1.at[1], dev(xx=x3), "gw")
     weight_grad(3, gwp.at[3])
-    send("gw_c", gwp.at[3, pl.ds(128, 128)], gw2.at[0, 1], dev(xx=x1), "gw")
+    send("gw2", gwp.at[3, pl.ds(128, 128)], gw2.at[0, 1], dev(xx=x1), "gw")
     weight_grad(1, gwp.at[1])
-    send("gw_d", gwp.at[1, pl.ds(0, 128)], gw2.at[1, 0], dev(xx=x3), "gw")
+    send("gw2", gwp.at[1, pl.ds(0, 128)], gw2.at[1, 0], dev(xx=x3), "gw")
     for step in (0, -1, 1, -2, 2):
         normed_grad_sum(step)
     normed_grad_sum(-3)
@@ -347,10 +341,10 @@
     pending["f"] = xb.at[pl.ds(0, 15)]
     arrived("gw_a", gw1.at[0])
     gws[0] = (gwp[3, 0:128].astype(F32) + gw1[0].astype(F32)).astype(BF16)
-    send("gw_e", gws.at[0], gw2.at[0, 0], dev(xx=x1), "gw")
+    send("gw2", gws.at[0], gw2.at[0, 0], dev(xx=x1), "gw")
     arrived("gw_b", gw1.at[1])
     gws[1] = (gwp[1, 128:256].astype(F32) + gw1[1].astype(F32)).astype(BF16)
-    send("gw_f", gws.at[1], gw2.at[1, 1], dev(xx=x3), "gw")
+    send("gw2", gws.at[1], gw2.at[1, 1], dev(xx=x3), "gw")
     weight_grad(0, gw_own)
     stores = [pltpu.make_async_copy(gw_own, own_hbm, store_sems.at[1])]
     stores[0].start()
@@ -379,10 +373,7 @@
     stores[0].wait()
     pltpu.make_async_copy(fk_keep, fk_keep, store_sems.at[0]).wait()
     arrived("fk", fk_send)
-    arrived("gw_c", gw2.at[0, 1])
-    arrived("gw_d", gw2.at[1, 0])
-    arrived("gw_e", gw2.at[0, 0])
-    arrived("gw_f", gw2.at[1, 1])
+    arrived("gw2", gw2)
     assert (len(send_names), len(recv_names)) == (N_SEND, N_RECV), (len(send_names), len(recv_names))
 
 

time: 57.9 us -> 57.9 us (level)
  no operation moved by 1% of the time
where the time goes in v6:
time: 57.9 us; the launch traced here: 57.8 us
  Pallas kernels  57.1 us (99%)
  between operations  0.64 us (1%)
    pallas_call x1, Pallas kernels, on_device(): pl.pallas_call(kernel, out_shape=(jax.ShapeDtypeStruct((NY, NZL, NK, 8, 2...  54.9 us
    pallas_call x1, Pallas kernels, on_device(): pl.pallas_call(finish, out_shape=(jax.ShapeDtypeStruct((8, 8192), BF16),...  2.28 us

profile of v6, /device:TPU:1, one launch (start us, length us, event | category | flops | bytes accessed | tf_op | source)
XLA Modules:
  0.0 57.8 jit_solution(4122350089680849651)
XLA Ops:
  0.6 54.9 %qkv_backward.1 = (f32[8,2,2,8,256]{4,3,2,1,0:T(8,128)}, f32[256,384]{1,0:T(8,128)}, bf16[2,2,128,384]{3,2,1,0:T(8,128)(2,1)}) custom-call(bf16[8,8192]{1,0:T(8,128)(2,1)} %x_ref.1, f32[1,8192]{1,0:T(1,128)} %bitcast.2, bf16[256,128]{1,0:T(8,128)(2,1)} %kvw_hbm.1, bf16[256,256]{1,0:T(8,128)(2,1)} %qw_hbm.1, bf16[128,256]{1,0:T(8,128)(2,1)} %bitcast.4, ...), custom_call_target="tpu_custom_call" | custom-call | flops 1700000000 | bytes 2000000 | tf_op jit(solution)/shard_map/qkv_backward/pallas_call | solution.py:409
  55.5 2.3 %finish.1 = (bf16[8,8192]{1,0:T(8,128)(2,1)}, f32[256,128]{1,0:T(8,128)}, f32[256,256]{1,0:T(8,128)}) custom-call(bf16[8,8192]{1,0:T(8,128)(2,1)} %x_ref.1, f32[1,8192]{1,0:T(1,128)} %bitcast.3, f32[8,2,2,8,256]{4,3,2,1,0:T(8,128)} %get-tuple-element.6.dn_ref, f32[256,384]{1,0:T(8,128)} %get-tuple-element.7.own_ref, ...), custom_call_target="tpu_custom_call" | custom-call | tf_op jit(solution)/shard_map/finish/pallas_call | solution.py:443
